TPU v7x, 32 devices: a whole 2x2x4 slice. The times are simulated.
32 devices in a mesh: blk: 8 (over z, y), group: 4 (over x, core).
Axes of the slice: x: 2, y: 2, z: 4, core: 2. Of those that a mesh axis runs over, the one named last changes fastest.
Arguments:
- image_embeds: bfloat16 [4, 768, 1152], P('group', 'blk')
- text_embeds: bfloat16 [4, 768, 1152], P('group', 'blk'), may hold values from -0.1875 to 0.1875
- positives: int32 [4, 768], P('group', 'blk'), may hold values from 0 to 767, each once within a row
- partner: int32 [4], replicated, may hold values from 0 to 3, each once
- log_temp: float32 [1], replicated, may hold values from 1.6 to 2.4
- bias: float32 [1], replicated, may hold values from -4 to -2
Outputs:
- image_grads: float32 [4, 768, 1152], P('group', 'blk')
- text_grads: float32 [4, 768, 1152], P('group', 'blk')
- loss: float32 [1], replicated
Inputs may be any that keep to these rules, and one draw needn't show every extreme that they name: Each group's positives name every text row of its partner group exactly once. `partner`: every group is named exactly once.
All inputs are finite; a program needn't handle non-finite values.
Results may differ from a plain program's by a relative error of at most 0.0015.
Values may be sent and summed in bfloat16 or wider, within the bound.
No kernel may reach another device: no remote copies, remote signals or barrier semaphores. Data moves between devices by JAX's collectives and lax.ppermute only.
A program may use at most 64 MiB of HBM per device.

v0:
```python
import functools

import jax
import jax.numpy as jnp
from jax import lax
from jax.experimental import pallas as pl
from jax.experimental.pallas import tpu as pltpu
from jax.sharding import PartitionSpec as P

TAIL = 16
DIGIT = 128
LANES = 128


def pair_slopes(rows, others, hits, temper, offset):
    logits = temper * jnp.dot(rows, others.T, preferred_element_type=jnp.float32) + offset
    hit_values = hits.astype(jnp.float32)
    slopes = (jax.nn.sigmoid(logits) - hit_values).astype(jnp.bfloat16)
    return logits, hit_values, slopes


def exchange(array, axis, size, mate):
    return lax.ppermute(array, axis, [(place, mate(place)) for place in range(size)])


def swap(array, axis, size, bit):
    return exchange(array, axis, size, lambda place: place ^ bit)


def after(array, *earlier):
    return lax.optimization_barrier((array, *earlier))[0]


def entry(partner, group):
    lane = lax.broadcasted_iota(jnp.int32, partner.shape, 1)
    return jnp.sum(jnp.where(lane == group, partner[...], 0), axis=1, keepdims=True)


def position(partner, group):
    lane = lax.broadcasted_iota(jnp.int32, partner.shape, 1)
    return jnp.sum(jnp.where(partner[...] == group, lane, 0), axis=1, keepdims=True)


def same_chip(group, other):
    return (group ^ other) >> 1 == 0


def offer_kernel(partner, own, across, out):
    here = lax.axis_index("group")
    out[...] = jnp.where(same_chip(entry(partner, here ^ 1), here), own[...], across[...])


def choose_kernel(partner, own, across, offered, out):
    here = lax.axis_index("group")
    wanted = entry(partner, here)
    held = jnp.where(same_chip(wanted, here), own[...], across[...])
    out[...] = jnp.where((wanted ^ here) & 1 == 0, held, offered[...])


def scorer_kernel(partner, every, out):
    wanted = position(partner, lax.axis_index("group"))
    found = every[0]
    for group in range(1, every.shape[0]):
        found = jnp.where(wanted == group, every[group], found)
    out[...] = found


LINE = (0, 4, 2, 6)


def with_labels(images, labels):
    digits = jnp.stack([labels // DIGIT, labels % DIGIT]).astype(images.dtype)
    return jnp.concatenate([images, jnp.pad(digits, ((0, TAIL - 2), (0, images.shape[1] - labels.shape[0])))])


def labels_of(block, rows, width):
    digits = block[rows : rows + TAIL, :width].astype(jnp.int32)
    return digits[:1] * DIGIT + digits[1:2]


def rows_by_rows(left, right):
    return lax.dot_general(left, right, (((1,), (1,)), ((), ())), preferred_element_type=jnp.float32)


def stack(blocks, rows, into):
    for place, block in enumerate(blocks):
        into[place * rows : (place + 1) * rows, :] = block[:rows, :]


def image_kernel(settings, images, mate, *refs):
    texts, (own_part, mate_part, loss, all_images, all_texts) = refs[:-5], refs[-5:]
    rows = texts[0].shape[0]
    temper = jnp.exp(settings[:, :1])
    stack((images, mate), rows, all_images)
    stack(texts, rows, all_texts)
    labels = jnp.concatenate([jnp.broadcast_to(labels_of(block, rows, LANES), (LANES, LANES)).T[:rows] for block in (images, mate)])
    labels = jnp.concatenate([labels] * (all_texts.shape[0] // LANES), axis=1)
    column = lax.broadcasted_iota(jnp.int32, labels.shape, 1)
    index = column
    for place, flip in enumerate(LINE):
        start = place * rows
        index = jnp.where(column >= start, column - start + (lax.axis_index("blk") ^ flip) * rows, index)

    logits = temper * rows_by_rows(all_images[...], all_texts[...]) + settings[:, 1:2]
    hit_values = (index == labels).astype(jnp.float32)
    small = jnp.exp(-jnp.abs(logits))
    losses = jnp.maximum(logits, 0.0) + jnp.log1p(small) - hit_values * logits
    slopes = jnp.where(logits >= 0.0, 1.0, small) / (1.0 + small) - hit_values
    total = losses.reshape(-1, 8, losses.shape[1]).sum(axis=0)
    loss[...] = sum(total[:, lane : lane + LANES] for lane in range(0, total.shape[1], LANES))
    grads = temper * jnp.dot(slopes.astype(jnp.bfloat16), all_texts[...], preferred_element_type=jnp.float32)
    own_part[...] = grads[:rows]
    mate_part[...] = grads[rows:]


def text_kernel(flip, count, settings, texts, *refs):
    images, earlier, part = refs[:count], refs[count:-1], refs[-1]
    rows = texts.shape[0]
    temper = jnp.exp(settings[:, :1])
    index = (lax.axis_index("blk") ^ flip) * rows + lax.broadcasted_iota(jnp.int32, (rows, rows), 0)
    total = jnp.zeros(part.shape, jnp.float32)
    for block in images:
        products = rows_by_rows(texts[...], block[:rows, :])
        hits = index == labels_of(block, rows, rows)
        slopes = (jax.nn.sigmoid(temper * products + settings[:, 1:2]) - hits.astype(jnp.float32)).astype(jnp.bfloat16)
        total += jnp.dot(slopes, block[:rows, :], preferred_element_type=jnp.float32)
    part[...] = temper * total + earlier[0][...] if earlier else temper * total


def finish_kernel(own_text, arrived, first, rest, text_grads, image_grads):
    rows, cut = own_text.shape[0], first.shape[0]
    text_grads[...] = own_text[...] + arrived[:rows]
    image_grads[:cut] = first[...]
    image_grads[cut:] = rest[...] + arrived[rows:]


def call(kernel, arrays, shapes, name, dtype=jnp.float32, scratch=()):
    return pl.pallas_call(
        kernel,
        out_shape=[jax.ShapeDtypeStruct(shape, dtype) for shape in shapes],
        in_specs=[pl.BlockSpec(memory_space=pltpu.VMEM)] * len(arrays),
        out_specs=[pl.BlockSpec(memory_space=pltpu.VMEM)] * len(shapes),
        scratch_shapes=[pltpu.VMEM(shape, jnp.bfloat16) for shape in scratch],
        compiler_params=pltpu.CompilerParams(vmem_limit_bytes=16 * 2**20),
        name=name,
    )(*arrays)


def hop_sum(total, hops):
    for axis, size, bit in hops:
        total = total + swap(total, axis, size, bit)
    return total


def shards(image_embeds, text_embeds, positives, partner, log_temp, bias):
    texts = text_embeds[0]
    labels = positives[0]
    rows = texts.shape[0]
    blocks = lax.axis_size("blk")
    groups = lax.axis_size("group")
    blk_place = lax.axis_index("blk")
    images = with_labels(image_embeds[0], labels)

    def index_of(places):
        return (jnp.stack(places)[:, None] * rows + jnp.arange(rows)[None, :]).reshape(-1)

    def matches(some_labels, index):
        return some_labels[:, None] == index[None, :]

    def grads(slopes, others):
        return temper * jnp.dot(slopes, others, preferred_element_type=jnp.float32)

    settings = jnp.concatenate([log_temp, bias]).reshape(1, 2)
    packed = after(jnp.concatenate([images, texts]), settings)
    tailed = images.shape[0]
    own_images, own_texts = packed[:rows], packed[tailed:]
    hops = [("group", groups, 1 << step) for step in range(groups.bit_length() - 1)]
    hops += [("blk", blocks, 1 << step) for step in range(blocks.bit_length() - 1)]
    choice = partner.reshape(1, groups)
    texts_across = swap(texts, "group", groups, 2)
    offer = call(offer_kernel, [choice, own_texts, texts_across], [texts.shape], "offer", texts.dtype)[0]
    offered = swap(offer, "group", groups, 1)
    partner_text = call(choose_kernel, [choice, own_texts, texts_across, offered], [texts.shape], "choose", texts.dtype)[0]
    group_images = lax.all_gather(after(packed[:tailed], partner_text), "group")
    scorer_image = call(scorer_kernel, [choice, group_images], [images.shape], "scorer", images.dtype)[0]

    if blocks == 8:

        def along(array, flip):
            return swap(array, "blk", blocks, flip)

        mate = along(packed, 1)
        text_two_off = along(partner_text, 4)
        text_one_off = along(partner_text, 2)
        text_three_off = along(after(text_two_off, text_one_off, mate, scorer_image), 2)
        image_one_off = along(after(scorer_image, text_three_off), 2)
        image_two_off = along(scorer_image, 4)
        column_texts = [partner_text, text_two_off, text_one_off, after(text_three_off, image_two_off)]
        grad_shape = texts.shape
        own_part, mate_part, total = call(
            image_kernel,
            [settings, packed[:tailed], mate[:tailed], *column_texts],
            [grad_shape, grad_shape, (8, LANES)],
            "image_side",
            scratch=[(2 * rows, texts.shape[1]), (len(LINE) * rows, texts.shape[1])],
        )
        image_three_off = along(image_two_off, 2)
        cut = rows * 5 // 6
        first_grads = own_part[:cut] + along(mate_part[:cut], 1)
        rest_own, rest = own_part[cut:], mate_part[cut:]
        total = hop_sum(total, hops[:2])
        total = hop_sum(after(total, image_one_off), hops[2:3])
        early_images = [scorer_image, image_two_off, image_one_off]
        early_part = call(functools.partial(text_kernel, 1, 3), [settings, mate[tailed:], *early_images], [grad_shape], "text_side_early")[0]
        last_image = after(image_three_off, total, early_part)
        mate_part = call(functools.partial(text_kernel, 1, 1), [settings, mate[tailed:], last_image, early_part], [grad_shape], "text_side_mate")[0]
        column_images = early_images + [last_image]
        arrived = along(jnp.concatenate([mate_part, rest]), 1)
        own_part = call(functools.partial(text_kernel, 0, 4), [settings, own_texts, *column_images], [grad_shape], "text_side_own")[0]
        text_grads, image_grads = call(
            finish_kernel, [own_part, arrived, first_grads, rest_own], [grad_shape, grad_shape], "finish"
        )
        total = after(hop_sum(after(total, first_grads), hops[3:4]), own_part)
        hops = hops[4:]
    else:
        temper = jnp.exp(log_temp[0])
        offset = bias[0]
        all_texts = lax.all_gather(partner_text, "blk", axis=0, tiled=True)
        every_image = lax.all_gather(scorer_image, "blk", axis=0)
        hits = matches(labels, jnp.arange(blocks * rows))
        logits, hit_values, slopes = pair_slopes(own_images, all_texts, hits, temper, offset)
        total = jnp.sum(jax.nn.softplus(logits) - hit_values * logits)
        total = jnp.zeros((8, 128)).at[0, 0].set(total)
        image_grads = grads(slopes, all_texts)
        all_images = every_image[:, :rows].reshape(blocks * rows, -1)
        back_labels = jax.vmap(lambda block: labels_of(block, rows, rows)[0])(every_image).reshape(-1)
        back_hits = matches(index_of([blk_place]), back_labels)
        back_slopes = pair_slopes(own_texts, all_images, back_hits, temper, offset)[2]
        text_grads = grads(back_slopes, all_images)

    total = hop_sum(total, hops)
    loss = jnp.sum(total * (1.0 / (groups * rows * blocks * blocks))).reshape(1)
    return (image_grads[None], text_grads[None], loss)


def solution(mesh):
    in_specs = (P("group", "blk", None), P("group", "blk", None), P("group", "blk"), P(), P(), P())
    out_specs = (P("group", "blk", None), P("group", "blk", None), P())
    return jax.shard_map(shards, mesh=mesh, in_specs=in_specs, out_specs=out_specs, check_vma=False)
```

profile of v0, /device:TPU:0, one launch (start us, length us, event | category | flops | bytes accessed | tf_op | source)
XLA Modules:
  0.0 66.8 jit_solution(3351947229198074521)
XLA Ops:
  0.6 3.0 %collective-permute-start = (bf16[96,1152]{1,0:T(8,128)(2,1)}, bf16[96,1152]{1,0:T(8,128)(2,1)S(1)}, u32[]{:S(2)}, u32[]{:S(2)}) collective-permute-start(bf16[96,1152]{1,0:T(8,128)(2,1)} %bitcast.14), channel_id=1, source_target_pairs={{0,2},{1,3},{2,0},{3,1},{4,6},{5,7},{6,4},{7,5},{8,10},{9,11},{10,... | collective-permute-start | bytes 663560 | tf_op jit(solution)/shard_map/ppermute | solution.py:23
  4.3 0.0 copy-start.1
  5.0 0.0 copy-done.1
  5.0 0.1 maximum_bitcast_fusion.settings
  5.1 1.1 %pad_maximum_fusion.1 = bf16[208,1152]{1,0:T(8,128)(2,1)S(1)} fusion(bf16[96,1152]{1,0:T(8,128)(2,1)} %bitcast.15, bf16[16,1152]{1,0:T(8,128)(2,1)S(1)} %fusion.5, bf16[96,1152]{1,0:T(8,128)(2,1)} %bitcast.13), kind=kLoop, calls=%fused_computation.1 | loop fusion | flops 1437696 | bytes 958464 | tf_op jit(solution)/shard_map/concatenate | solution.py:174
  6.2 0.0 copy-start
  6.2 3.1 %collective-permute-done.across = bf16[96,1152]{1,0:T(8,128)(2,1)S(1)} collective-permute-done((bf16[96,1152]{1,0:T(8,128)(2,1)}, bf16[96,1152]{1,0:T(8,128)(2,1)S(1)}, u32[]{:S(2)}, u32[]{:S(2)}) %collective-permute-start) | collective-permute-done | bytes 221216 | tf_op jit(solution)/shard_map/ppermute | solution.py:23
  9.3 0.1 offer.1
  9.4 0.1 collective-permute-start.1
  9.5 1.8 %collective-permute-start.5 = (bf16[208,1152]{1,0:T(8,128)(2,1)S(1)}, bf16[208,1152]{1,0:T(8,128)(2,1)S(1)}, u32[]{:S(2)}, u32[]{:S(2)}) collective-permute-start(bf16[208,1152]{1,0:T(8,128)(2,1)S(1)} %pad_maximum_fusion.1), channel_id=1, source_target_pairs={{0,4},{4,0},{8,12},{12,8},{16,20},{20,16},{24,28},{28,24},{1,5},{5... | collective-permute-start | bytes 1437704 | tf_op jit(solution)/shard_map/ppermute | solution.py:23
  11.3 0.0 collective-permute-done.1.offered
  11.3 0.1 choose.1.refs_0_
  11.5 1.6 %collective-permute-start.4 = (bf16[96,1152]{1,0:T(8,128)(2,1)S(1)}, bf16[96,1152]{1,0:T(8,128)(2,1)S(1)}, u32[]{:S(2)}, u32[]{:S(2)}) collective-permute-start(bf16[96,1152]{1,0:T(8,128)(2,1)S(1)} %choose.1.refs_0_), channel_id=1, source_target_pairs={{0,8},{4,12},{8,0},{12,4},{16,24},{20,28},{24,16},{28,20},{1,9},{5... | collective-permute-start | bytes 663560 | tf_op jit(solution)/shard_map/ppermute | solution.py:23
  13.1 2.6 %collective-permute-start.3 = (bf16[96,1152]{1,0:T(8,128)(2,1)S(1)}, bf16[96,1152]{1,0:T(8,128)(2,1)S(1)}, u32[]{:S(2)}, u32[]{:S(2)}) collective-permute-start(bf16[96,1152]{1,0:T(8,128)(2,1)S(1)} %choose.1.refs_0_), channel_id=1, source_target_pairs={{0,16},{4,20},{8,24},{12,28},{16,0},{20,4},{24,8},{28,12},{1,17},{... | collective-permute-start | bytes 663560 | tf_op jit(solution)/shard_map/ppermute | solution.py:23
  15.7 9.9 %all-gather = bf16[448,1152]{1,0:T(8,128)(2,1)S(1)} all-gather(bf16[112,1152]{1,0:T(8,128)(2,1)S(1)} %slice.27.images), channel_id=2, replica_groups=mesh['blk'=8,'group'=4] {'group'}, dimensions={0}, use_global_device_ids=true | all-gather | bytes 1290240 | tf_op jit(solution)/shard_map/all_gather | solution.py:184
  25.6 0.2 scorer.1.refs_0_
  25.8 0.4 collective-permute-start.2
  26.2 0.0 collective-permute-done.5
  26.2 0.0 collective-permute-done.4.refs_2_
  26.2 0.0 collective-permute-done.3.refs_1_
  26.2 0.5 collective-permute-start.6
  26.7 10.3 %collective-permute-done.6.refs_3_ = bf16[96,1152]{1,0:T(8,128)(2,1)S(1)} collective-permute-done((bf16[96,1152]{1,0:T(8,128)(2,1)S(1)}, bf16[96,1152]{1,0:T(8,128)(2,1)S(1)}, u32[]{:S(2)}, u32[]{:S(2)}) %collective-permute-start.6) | collective-permute-done | bytes 221216 | tf_op jit(solution)/shard_map/ppermute | solution.py:23
  37.0 2.5 %collective-permute-start.7 = (bf16[112,1152]{1,0:T(8,128)(2,1)S(1)}, bf16[112,1152]{1,0:T(8,128)(2,1)S(1)}, u32[]{:S(2)}, u32[]{:S(2)}) collective-permute-start(bf16[112,1152]{1,0:T(8,128)(2,1)S(1)} %scorer.1.refs_0_), channel_id=1, source_target_pairs={{0,8},{4,12},{8,0},{12,4},{16,24},{20,28},{24,16},{28,20},{1,9},{5... | collective-permute-start | bytes 774152 | tf_op jit(solution)/shard_map/ppermute | solution.py:23
  39.5 1.3 %collective-permute-done.2.refs_1_ = bf16[112,1152]{1,0:T(8,128)(2,1)S(1)} collective-permute-done((bf16[112,1152]{1,0:T(8,128)(2,1)S(1)}, bf16[112,1152]{1,0:T(8,128)(2,1)S(1)}, u32[]{:S(2)}, u32[]{:S(2)}) %collective-permute-start.2) | collective-permute-done | bytes 258080 | tf_op jit(solution)/shard_map/ppermute | solution.py:23
  40.7 0.0 collective-permute-start.8
  40.8 1.0 %image_side.1 = (f32[96,1152]{1,0:T(8,128)S(1)}, f32[96,1152]{1,0:T(8,128)S(1)}, f32[8,128]{1,0:T(8,128)S(1)}) custom-call(f32[1,2]{1,0:T(1,128)S(1)} %maximum_bitcast_fusion.settings, bf16[112,1152]{1,0:T(8,128)(2,1)S(1)} %slice.27.images, bf16[112,1152]{1,0:T(8,128)(2,1)S(1)} %slice.34.mate, bf16[96,1152]{1,0:T(8,128)(2,1)S(1)} %choose.1.refs_0_, ...), custom_call_target="tpu_custom_call" | custom-call | tf_op jit(solution)/shard_map/image_side/pallas_call | solution.py:138
  41.9 1.4 %collective-permute-start.13 = (f32[80,1152]{1,0:T(8,128)S(1)}, f32[80,1152]{1,0:T(8,128)S(1)}, u32[]{:S(2)}, u32[]{:S(2)}) collective-permute-start(f32[80,1152]{1,0:T(8,128)S(1)} %slice.32), channel_id=1, source_target_pairs={{0,4},{4,0},{8,12},{12,8},{16,20},{20,16},{24,28},{28,24},{1,5},{5... | collective-permute-start | bytes 1105928 | tf_op jit(solution)/shard_map/ppermute | solution.py:23
  43.3 0.0 collective-permute-start.9
  43.3 1.2 %collective-permute-done.9 = f32[8,128]{1,0:T(8,128)S(1)} collective-permute-done((f32[8,128]{1,0:T(8,128)S(1)}, f32[8,128]{1,0:T(8,128)S(1)}, u32[]{:S(2)}, u32[]{:S(2)}) %collective-permute-start.9) | collective-permute-done | bytes 4128 | tf_op jit(solution)/shard_map/ppermute | solution.py:23
  44.5 0.8 %collective-permute-start.10 = (f32[8,128]{1,0:T(8,128)S(1)}, f32[8,128]{1,0:T(8,128)S(1)}, u32[]{:S(2)}, u32[]{:S(2)}) collective-permute-start(f32[8,128]{1,0:T(8,128)S(1)} %add.30), channel_id=1, source_target_pairs={{0,2},{1,3},{2,0},{3,1},{4,6},{5,7},{6,4},{7,5},{8,10},{9,11},{10,... | collective-permute-start | bytes 12296 | tf_op jit(solution)/shard_map/ppermute | solution.py:23
  45.3 2.8 %collective-permute-done.10 = f32[8,128]{1,0:T(8,128)S(1)} collective-permute-done((f32[8,128]{1,0:T(8,128)S(1)}, f32[8,128]{1,0:T(8,128)S(1)}, u32[]{:S(2)}, u32[]{:S(2)}) %collective-permute-start.10) | collective-permute-done | bytes 4128 | tf_op jit(solution)/shard_map/ppermute | solution.py:23
  48.1 0.0 collective-permute-done.7.refs_2_
  48.1 0.7 collective-permute-start.11
  48.8 0.8 %text_side_early.1.refs_1_ = f32[96,1152]{1,0:T(8,128)S(1)} custom-call(f32[1,2]{1,0:T(1,128)S(1)} %maximum_bitcast_fusion.settings, bf16[96,1152]{1,0:T(8,128)(2,1)S(1)} %slice.35.texts, bf16[112,1152]{1,0:T(8,128)(2,1)S(1)} %scorer.1.refs_0_, bf16[112,1152]{1,0:T(8,128)(2,1)S(1)} %collective-permute-done.2.refs_1_, ...), custom_call_target="tpu_custom_call" | custom-call | tf_op jit(solution)/shard_map/text_side_early/pallas_call | solution.py:138
  49.6 2.9 %collective-permute-done.11 = f32[8,128]{1,0:T(8,128)S(1)} collective-permute-done((f32[8,128]{1,0:T(8,128)S(1)}, f32[8,128]{1,0:T(8,128)S(1)}, u32[]{:S(2)}, u32[]{:S(2)}) %collective-permute-start.11) | collective-permute-done | bytes 4128 | tf_op jit(solution)/shard_map/ppermute | solution.py:23
  52.5 0.0 collective-permute-done.8.refs_3_.refs_0_
  52.5 0.5 text_side_mate.1
  53.0 1.4 %collective-permute-start.12 = (f32[112,1152]{1,0:T(8,128)S(1)}, f32[112,1152]{1,0:T(8,128)S(1)}, u32[]{:S(2)}, u32[]{:S(2)}) collective-permute-start(f32[112,1152]{1,0:T(8,128)S(1)} %pad_maximum_fusion), channel_id=1, source_target_pairs={{0,4},{4,0},{8,12},{12,8},{16,20},{20,16},{24,28},{28,24},{1,5},{5... | collective-permute-start | bytes 1548296 | tf_op jit(solution)/shard_map/ppermute | solution.py:23
  54.4 0.0 collective-permute-done.13
  54.4 0.1 slice_add_fusion.first
  54.5 1.8 %collective-permute-start.14 = (f32[8,128]{1,0:T(8,128)S(1)}, f32[8,128]{1,0:T(8,128)S(1)}, u32[]{:S(2)}, u32[]{:S(2)}) collective-permute-start(f32[8,128]{1,0:T(8,128)S(1)} %add.32), channel_id=1, source_target_pairs={{0,8},{4,12},{8,0},{12,4},{16,24},{20,28},{24,16},{28,20},{1,9},{5... | collective-permute-start | bytes 12296 | tf_op jit(solution)/shard_map/ppermute | solution.py:23
  56.3 1.1 %text_side_own.1.own_text = f32[96,1152]{1,0:T(8,128)S(1)} custom-call(f32[1,2]{1,0:T(1,128)S(1)} %maximum_bitcast_fusion.settings, bf16[96,1152]{1,0:T(8,128)(2,1)S(1)} %slice.26.own.texts, bf16[112,1152]{1,0:T(8,128)(2,1)S(1)} %scorer.1.refs_0_, bf16[112,1152]{1,0:T(8,128)(2,1)S(1)} %collective-permute-done.2.refs_1_, ...), custom_call_target="tpu_custom_call" | custom-call | tf_op jit(solution)/shard_map/text_side_own/pallas_call | solution.py:138
  57.4 0.7 %collective-permute-done.14 = f32[8,128]{1,0:T(8,128)S(1)} collective-permute-done((f32[8,128]{1,0:T(8,128)S(1)}, f32[8,128]{1,0:T(8,128)S(1)}, u32[]{:S(2)}, u32[]{:S(2)}) %collective-permute-start.14) | collective-permute-done | bytes 4128 | tf_op jit(solution)/shard_map/ppermute | solution.py:23
  58.2 1.2 %collective-permute-start.15 = (f32[8,128]{1,0:T(8,128)S(1)}, f32[8,128]{1,0:T(8,128)S(1)}, u32[]{:S(2)}, u32[]{:S(2)}) collective-permute-start(f32[8,128]{1,0:T(8,128)S(1)} %add.34), channel_id=1, source_target_pairs={{0,16},{4,20},{8,24},{12,28},{16,0},{20,4},{24,8},{28,12},{1,17},{... | collective-permute-start | bytes 12296 | tf_op jit(solution)/shard_map/ppermute | solution.py:23
  59.4 3.3 %collective-permute-done.15 = f32[8,128]{1,0:T(8,128)S(1)} collective-permute-done((f32[8,128]{1,0:T(8,128)S(1)}, f32[8,128]{1,0:T(8,128)S(1)}, u32[]{:S(2)}, u32[]{:S(2)}) %collective-permute-start.15) | collective-permute-done | bytes 4128 | tf_op jit(solution)/shard_map/ppermute | solution.py:23
  62.7 0.6 multiply_reduce_fusion
  63.3 2.6 %collective-permute-done.12.arrived = f32[112,1152]{1,0:T(8,128)S(1)} collective-permute-done((f32[112,1152]{1,0:T(8,128)S(1)}, f32[112,1152]{1,0:T(8,128)S(1)}, u32[]{:S(2)}, u32[]{:S(2)}) %collective-permute-start.12) | collective-permute-done | bytes 516128 | tf_op jit(solution)/shard_map/ppermute | solution.py:23
  65.8 1.0 %finish.1 = (f32[96,1152]{1,0:T(8,128)}, f32[96,1152]{1,0:T(8,128)}) custom-call(f32[96,1152]{1,0:T(8,128)S(1)} %text_side_own.1.own_text, f32[112,1152]{1,0:T(8,128)S(1)} %collective-permute-done.12.arrived, f32[80,1152]{1,0:T(8,128)S(1)} %slice_add_fusion.first, f32[16,1152]{1,0:T(8,128)S(1)} %slice.33.rest), custom_call_target="tpu_custom_call" | custom-call | tf_op jit(solution)/shard_map/finish/pallas_call | solution.py:138
  (15 shorter events, 0.2 us)
Async XLA Ops:
  0.6 8.6 %collective-permute-start = (bf16[96,1152]{1,0:T(8,128)(2,1)}, bf16[96,1152]{1,0:T(8,128)(2,1)S(1)}, u32[]{:S(2)}, u32[]{:S(2)}) collective-permute-start(bf16[96,1152]{1,0:T(8,128)(2,1)} %bitcast.14), channel_id=1, source_target_pairs={{0,2},{1,3},{2,0},{3,1},{4,6},{5,7},{6,4},{7,5},{8,10},{9,11},{10,... | collective-permute-start | bytes 663560 | tf_op jit(solution)/shard_map/ppermute | solution.py:23
  4.3 0.7 %copy-start.1 = (s32[1,96]{1,0:T(1,128)S(1)}, s32[1,96]{1,0:T(1,128)}, u32[]{:S(2)}) copy-start(s32[1,96]{1,0:T(1,128)} %param.8) | copy-start | bytes 1156
  6.2 3.1 %copy-start = (s32[4]{0:T(128)S(1)}, s32[4]{0:T(128)}, u32[]{:S(2)}) copy-start(s32[4]{0:T(128)} %param.9) | copy-start | bytes 52
  9.4 1.9 %collective-permute-start.1 = (bf16[96,1152]{1,0:T(8,128)(2,1)S(1)}, bf16[96,1152]{1,0:T(8,128)(2,1)S(1)}, u32[]{:S(2)}, u32[]{:S(2)}) collective-permute-start(bf16[96,1152]{1,0:T(8,128)(2,1)S(1)} %offer.1), channel_id=1, source_target_pairs={{0,1},{1,0},{2,3},{3,2},{4,5},{5,4},{6,7},{7,6},{8,9},{9,8},{10,11... | collective-permute-start | bytes 663560 | tf_op jit(solution)/shard_map/ppermute | solution.py:23
  9.5 16.7 %collective-permute-start.5 = (bf16[208,1152]{1,0:T(8,128)(2,1)S(1)}, bf16[208,1152]{1,0:T(8,128)(2,1)S(1)}, u32[]{:S(2)}, u32[]{:S(2)}) collective-permute-start(bf16[208,1152]{1,0:T(8,128)(2,1)S(1)} %pad_maximum_fusion.1), channel_id=1, source_target_pairs={{0,4},{4,0},{8,12},{12,8},{16,20},{20,16},{24,28},{28,24},{1,5},{5... | collective-permute-start | bytes 1437704 | tf_op jit(solution)/shard_map/ppermute | solution.py:23
  11.5 14.7 %collective-permute-start.4 = (bf16[96,1152]{1,0:T(8,128)(2,1)S(1)}, bf16[96,1152]{1,0:T(8,128)(2,1)S(1)}, u32[]{:S(2)}, u32[]{:S(2)}) collective-permute-start(bf16[96,1152]{1,0:T(8,128)(2,1)S(1)} %choose.1.refs_0_), channel_id=1, source_target_pairs={{0,8},{4,12},{8,0},{12,4},{16,24},{20,28},{24,16},{28,20},{1,9},{5... | collective-permute-start | bytes 663560 | tf_op jit(solution)/shard_map/ppermute | solution.py:23
  13.1 13.1 %collective-permute-start.3 = (bf16[96,1152]{1,0:T(8,128)(2,1)S(1)}, bf16[96,1152]{1,0:T(8,128)(2,1)S(1)}, u32[]{:S(2)}, u32[]{:S(2)}) collective-permute-start(bf16[96,1152]{1,0:T(8,128)(2,1)S(1)} %choose.1.refs_0_), channel_id=1, source_target_pairs={{0,16},{4,20},{8,24},{12,28},{16,0},{20,4},{24,8},{28,12},{1,17},{... | collective-permute-start | bytes 663560 | tf_op jit(solution)/shard_map/ppermute | solution.py:23
  25.8 14.9 %collective-permute-start.2 = (bf16[112,1152]{1,0:T(8,128)(2,1)S(1)}, bf16[112,1152]{1,0:T(8,128)(2,1)S(1)}, u32[]{:S(2)}, u32[]{:S(2)}) collective-permute-start(bf16[112,1152]{1,0:T(8,128)(2,1)S(1)} %scorer.1.refs_0_), channel_id=1, source_target_pairs={{0,16},{4,20},{8,24},{12,28},{16,0},{20,4},{24,8},{28,12},{1,17},{... | collective-permute-start | bytes 774152 | tf_op jit(solution)/shard_map/ppermute | solution.py:23
  26.2 10.8 %collective-permute-start.6 = (bf16[96,1152]{1,0:T(8,128)(2,1)S(1)}, bf16[96,1152]{1,0:T(8,128)(2,1)S(1)}, u32[]{:S(2)}, u32[]{:S(2)}) collective-permute-start(bf16[96,1152]{1,0:T(8,128)(2,1)S(1)} %collective-permute-done.3.refs_1_), channel_id=1, source_target_pairs={{0,8},{4,12},{8,0},{12,4},{16,24},{20,28},{24,16},{28,20},{1,9},{5... | collective-permute-start | bytes 663560 | tf_op jit(solution)/shard_map/ppermute | solution.py:23
  37.0 11.1 %collective-permute-start.7 = (bf16[112,1152]{1,0:T(8,128)(2,1)S(1)}, bf16[112,1152]{1,0:T(8,128)(2,1)S(1)}, u32[]{:S(2)}, u32[]{:S(2)}) collective-permute-start(bf16[112,1152]{1,0:T(8,128)(2,1)S(1)} %scorer.1.refs_0_), channel_id=1, source_target_pairs={{0,8},{4,12},{8,0},{12,4},{16,24},{20,28},{24,16},{28,20},{1,9},{5... | collective-permute-start | bytes 774152 | tf_op jit(solution)/shard_map/ppermute | solution.py:23
  40.7 11.7 %collective-permute-start.8 = (bf16[112,1152]{1,0:T(8,128)(2,1)S(1)}, bf16[112,1152]{1,0:T(8,128)(2,1)S(1)}, u32[]{:S(2)}, u32[]{:S(2)}) collective-permute-start(bf16[112,1152]{1,0:T(8,128)(2,1)S(1)} %collective-permute-done.2.refs_1_), channel_id=1, source_target_pairs={{0,8},{4,12},{8,0},{12,4},{16,24},{20,28},{24,16},{28,20},{1,9},{5... | collective-permute-start | bytes 774152 | tf_op jit(solution)/shard_map/ppermute | solution.py:23
  41.9 12.6 %collective-permute-start.13 = (f32[80,1152]{1,0:T(8,128)S(1)}, f32[80,1152]{1,0:T(8,128)S(1)}, u32[]{:S(2)}, u32[]{:S(2)}) collective-permute-start(f32[80,1152]{1,0:T(8,128)S(1)} %slice.32), channel_id=1, source_target_pairs={{0,4},{4,0},{8,12},{12,8},{16,20},{20,16},{24,28},{28,24},{1,5},{5... | collective-permute-start | bytes 1105928 | tf_op jit(solution)/shard_map/ppermute | solution.py:23
  43.3 1.2 %collective-permute-start.9 = (f32[8,128]{1,0:T(8,128)S(1)}, f32[8,128]{1,0:T(8,128)S(1)}, u32[]{:S(2)}, u32[]{:S(2)}) collective-permute-start(f32[8,128]{1,0:T(8,128)S(1)} %get-tuple-element.22), channel_id=1, source_target_pairs={{0,1},{1,0},{2,3},{3,2},{4,5},{5,4},{6,7},{7,6},{8,9},{9,8},{10,11... | collective-permute-start | bytes 12296 | tf_op jit(solution)/shard_map/ppermute | solution.py:23
  44.5 3.6 %collective-permute-start.10 = (f32[8,128]{1,0:T(8,128)S(1)}, f32[8,128]{1,0:T(8,128)S(1)}, u32[]{:S(2)}, u32[]{:S(2)}) collective-permute-start(f32[8,128]{1,0:T(8,128)S(1)} %add.30), channel_id=1, source_target_pairs={{0,2},{1,3},{2,0},{3,1},{4,6},{5,7},{6,4},{7,5},{8,10},{9,11},{10,... | collective-permute-start | bytes 12296 | tf_op jit(solution)/shard_map/ppermute | solution.py:23
  48.1 4.4 %collective-permute-start.11 = (f32[8,128]{1,0:T(8,128)S(1)}, f32[8,128]{1,0:T(8,128)S(1)}, u32[]{:S(2)}, u32[]{:S(2)}) collective-permute-start(f32[8,128]{1,0:T(8,128)S(1)} %add.31), channel_id=1, source_target_pairs={{0,4},{4,0},{8,12},{12,8},{16,20},{20,16},{24,28},{28,24},{1,5},{5... | collective-permute-start | bytes 12296 | tf_op jit(solution)/shard_map/ppermute | solution.py:23
  53.0 12.8 %collective-permute-start.12 = (f32[112,1152]{1,0:T(8,128)S(1)}, f32[112,1152]{1,0:T(8,128)S(1)}, u32[]{:S(2)}, u32[]{:S(2)}) collective-permute-start(f32[112,1152]{1,0:T(8,128)S(1)} %pad_maximum_fusion), channel_id=1, source_target_pairs={{0,4},{4,0},{8,12},{12,8},{16,20},{20,16},{24,28},{28,24},{1,5},{5... | collective-permute-start | bytes 1548296 | tf_op jit(solution)/shard_map/ppermute | solution.py:23
  54.5 3.7 %collective-permute-start.14 = (f32[8,128]{1,0:T(8,128)S(1)}, f32[8,128]{1,0:T(8,128)S(1)}, u32[]{:S(2)}, u32[]{:S(2)}) collective-permute-start(f32[8,128]{1,0:T(8,128)S(1)} %add.32), channel_id=1, source_target_pairs={{0,8},{4,12},{8,0},{12,4},{16,24},{20,28},{24,16},{28,20},{1,9},{5... | collective-permute-start | bytes 12296 | tf_op jit(solution)/shard_map/ppermute | solution.py:23
  58.2 4.5 %collective-permute-start.15 = (f32[8,128]{1,0:T(8,128)S(1)}, f32[8,128]{1,0:T(8,128)S(1)}, u32[]{:S(2)}, u32[]{:S(2)}) collective-permute-start(f32[8,128]{1,0:T(8,128)S(1)} %add.34), channel_id=1, source_target_pairs={{0,16},{4,20},{8,24},{12,28},{16,0},{20,4},{24,8},{28,12},{1,17},{... | collective-permute-start | bytes 12296 | tf_op jit(solution)/shard_map/ppermute | solution.py:23
where the time goes:
time: 67 us; the launch traced here: 66.8 us
  waiting for transfers between devices  28 us (42%)
  starting transfers between devices  19.9 us (30%)
  blocking collectives  9.92 us (15%)
  Pallas kernels  4.9 us (7%)
  between operations  2.1 us (3%)
  other arithmetic  1.89 us (3%)
    ppermute x16, waiting for transfers between devices, exchange(): lax.ppermute(array, axis, [(place, mate(place)) for place in range(size)])  28 us
    ppermute x16, starting transfers between devices, exchange(): lax.ppermute(array, axis, [(place, mate(place)) for place in range(size)])  19.9 us
    all_gather x1, blocking collectives, shards(): group_images = lax.all_gather(after(packed[:tailed], partner_text), 'group')  9.92 us
    pallas_call x8, Pallas kernels, call(): pl.pallas_call(kernel, out_shape=[jax.ShapeDtypeStruct(shape, dtype) for...  4.9 us
  transfers between devices with their start and end apart: 16, of which 9 were waited for; matrix products, arithmetic and copies ran while one was open for 3% of the time, Pallas kernels for 6%

commit v1 on v0

--- a/solution.py
+++ b/solution.py
@@ -7,7 +7,7 @@
 from jax.experimental.pallas import tpu as pltpu
 from jax.sharding import PartitionSpec as P
 
-TAIL = 16
+TAIL = 8
 DIGIT = 128
 LANES = 128
 

time: 67 us -> 65.9 us (0.984)
  transfers between devices with their start and end apart: 16 -> 16, of which waited for: 9 -> 10; matrix products, arithmetic and copies ran while one was open for 3% -> 3% of each run, Pallas kernels for 6% -> 6%
where the time goes in v1:
time: 65.9 us; the launch traced here: 65.7 us
  waiting for transfers between devices  27.4 us (42%)
  starting transfers between devices  19.8 us (30%)
  blocking collectives  9.52 us (14%)
  Pallas kernels  4.88 us (7%)
  between operations  2.09 us (3%)
  other arithmetic  1.89 us (3%)
    ppermute x16, waiting for transfers between devices, exchange(): lax.ppermute(array, axis, [(place, mate(place)) for place in range(size)])  27.4 us
    ppermute x16, starting transfers between devices, exchange(): lax.ppermute(array, axis, [(place, mate(place)) for place in range(size)])  19.8 us
    all_gather x1, blocking collectives, shards(): group_images = lax.all_gather(after(packed[:tailed], partner_text), 'group')  9.52 us
    pallas_call x8, Pallas kernels, call(): pl.pallas_call(kernel, out_shape=[jax.ShapeDtypeStruct(shape, dtype) for...  4.88 us
  transfers between devices with their start and end apart: 16, of which 10 were waited for; matrix products, arithmetic and copies ran while one was open for 3% of the time, Pallas kernels for 6%

profile of v1, /device:TPU:0, one launch (start us, length us, event | category | flops | bytes accessed | tf_op | source)
XLA Modules:
  0.0 65.7 jit_solution(5890238567449017522)
XLA Ops:
  0.6 3.0 %collective-permute-start = (bf16[96,1152]{1,0:T(8,128)(2,1)}, bf16[96,1152]{1,0:T(8,128)(2,1)S(1)}, u32[]{:S(2)}, u32[]{:S(2)}) collective-permute-start(bf16[96,1152]{1,0:T(8,128)(2,1)} %bitcast.14), channel_id=1, source_target_pairs={{0,2},{1,3},{2,0},{3,1},{4,6},{5,7},{6,4},{7,5},{8,10},{9,11},{10,... | collective-permute-start | bytes 663560 | tf_op jit(solution)/shard_map/ppermute | solution.py:23
  5.0 0.0 copy-done.1
  5.0 0.1 maximum_bitcast_fusion.settings
  5.1 1.1 %pad_maximum_fusion.1 = bf16[200,1152]{1,0:T(8,128)(2,1)S(1)} fusion(bf16[96,1152]{1,0:T(8,128)(2,1)} %bitcast.15, bf16[8,1152]{1,0:T(8,128)(2,1)S(1)} %fusion.5, bf16[96,1152]{1,0:T(8,128)(2,1)} %bitcast.13), kind=kLoop, calls=%fused_computation.1 | loop fusion | flops 1382400 | bytes 921600 | tf_op jit(solution)/shard_map/concatenate | solution.py:174
  6.2 0.0 copy-start
  6.2 3.1 %collective-permute-done.across = bf16[96,1152]{1,0:T(8,128)(2,1)S(1)} collective-permute-done((bf16[96,1152]{1,0:T(8,128)(2,1)}, bf16[96,1152]{1,0:T(8,128)(2,1)S(1)}, u32[]{:S(2)}, u32[]{:S(2)}) %collective-permute-start) | collective-permute-done | bytes 221216 | tf_op jit(solution)/shard_map/ppermute | solution.py:23
  9.3 0.0 copy-done
  9.3 0.1 offer.1
  9.4 0.1 collective-permute-start.1
  9.5 1.8 %collective-permute-start.5 = (bf16[200,1152]{1,0:T(8,128)(2,1)S(1)}, bf16[200,1152]{1,0:T(8,128)(2,1)S(1)}, u32[]{:S(2)}, u32[]{:S(2)}) collective-permute-start(bf16[200,1152]{1,0:T(8,128)(2,1)S(1)} %pad_maximum_fusion.1), channel_id=1, source_target_pairs={{0,4},{4,0},{8,12},{12,8},{16,20},{20,16},{24,28},{28,24},{1,5},{5... | collective-permute-start | bytes 1382408 | tf_op jit(solution)/shard_map/ppermute | solution.py:23
  11.3 0.0 collective-permute-done.1.offered
  11.3 0.1 choose.1.refs_0_
  11.5 1.6 %collective-permute-start.4 = (bf16[96,1152]{1,0:T(8,128)(2,1)S(1)}, bf16[96,1152]{1,0:T(8,128)(2,1)S(1)}, u32[]{:S(2)}, u32[]{:S(2)}) collective-permute-start(bf16[96,1152]{1,0:T(8,128)(2,1)S(1)} %choose.1.refs_0_), channel_id=1, source_target_pairs={{0,8},{4,12},{8,0},{12,4},{16,24},{20,28},{24,16},{28,20},{1,9},{5... | collective-permute-start | bytes 663560 | tf_op jit(solution)/shard_map/ppermute | solution.py:23
  13.1 2.6 %collective-permute-start.3 = (bf16[96,1152]{1,0:T(8,128)(2,1)S(1)}, bf16[96,1152]{1,0:T(8,128)(2,1)S(1)}, u32[]{:S(2)}, u32[]{:S(2)}) collective-permute-start(bf16[96,1152]{1,0:T(8,128)(2,1)S(1)} %choose.1.refs_0_), channel_id=1, source_target_pairs={{0,16},{4,20},{8,24},{12,28},{16,0},{20,4},{24,8},{28,12},{1,17},{... | collective-permute-start | bytes 663560 | tf_op jit(solution)/shard_map/ppermute | solution.py:23
  15.7 9.5 %all-gather = bf16[416,1152]{1,0:T(8,128)(2,1)S(1)} all-gather(bf16[104,1152]{1,0:T(8,128)(2,1)S(1)} %slice.27.images), channel_id=2, replica_groups=mesh['blk'=8,'group'=4] {'group'}, dimensions={0}, use_global_device_ids=true | all-gather | bytes 1198080 | tf_op jit(solution)/shard_map/all_gather | solution.py:184
  25.2 0.2 scorer.1.refs_0_
  25.4 0.4 collective-permute-start.2
  25.8 0.0 collective-permute-done.5
  25.8 0.0 collective-permute-done.4.refs_2_
  25.8 0.2 collective-permute-done.3.refs_1_
  26.0 0.4 collective-permute-start.6
  26.5 9.7 %collective-permute-done.6.refs_3_ = bf16[96,1152]{1,0:T(8,128)(2,1)S(1)} collective-permute-done((bf16[96,1152]{1,0:T(8,128)(2,1)S(1)}, bf16[96,1152]{1,0:T(8,128)(2,1)S(1)}, u32[]{:S(2)}, u32[]{:S(2)}) %collective-permute-start.6) | collective-permute-done | bytes 221216 | tf_op jit(solution)/shard_map/ppermute | solution.py:23
  36.2 2.5 %collective-permute-start.7 = (bf16[104,1152]{1,0:T(8,128)(2,1)S(1)}, bf16[104,1152]{1,0:T(8,128)(2,1)S(1)}, u32[]{:S(2)}, u32[]{:S(2)}) collective-permute-start(bf16[104,1152]{1,0:T(8,128)(2,1)S(1)} %scorer.1.refs_0_), channel_id=1, source_target_pairs={{0,8},{4,12},{8,0},{12,4},{16,24},{20,28},{24,16},{28,20},{1,9},{5... | collective-permute-start | bytes 718856 | tf_op jit(solution)/shard_map/ppermute | solution.py:23
  38.7 0.8 %collective-permute-done.2.refs_1_ = bf16[104,1152]{1,0:T(8,128)(2,1)S(1)} collective-permute-done((bf16[104,1152]{1,0:T(8,128)(2,1)S(1)}, bf16[104,1152]{1,0:T(8,128)(2,1)S(1)}, u32[]{:S(2)}, u32[]{:S(2)}) %collective-permute-start.2) | collective-permute-done | bytes 239648 | tf_op jit(solution)/shard_map/ppermute | solution.py:23
  39.5 0.0 collective-permute-start.8
  39.5 1.0 %image_side.1 = (f32[96,1152]{1,0:T(8,128)S(1)}, f32[96,1152]{1,0:T(8,128)S(1)}, f32[8,128]{1,0:T(8,128)S(1)}) custom-call(f32[1,2]{1,0:T(1,128)S(1)} %maximum_bitcast_fusion.settings, bf16[104,1152]{1,0:T(8,128)(2,1)S(1)} %slice.27.images, bf16[104,1152]{1,0:T(8,128)(2,1)S(1)} %slice.34.mate, bf16[96,1152]{1,0:T(8,128)(2,1)S(1)} %choose.1.refs_0_, ...), custom_call_target="tpu_custom_call" | custom-call | tf_op jit(solution)/shard_map/image_side/pallas_call | solution.py:138
  40.6 1.4 %collective-permute-start.13 = (f32[80,1152]{1,0:T(8,128)S(1)}, f32[80,1152]{1,0:T(8,128)S(1)}, u32[]{:S(2)}, u32[]{:S(2)}) collective-permute-start(f32[80,1152]{1,0:T(8,128)S(1)} %slice.32), channel_id=1, source_target_pairs={{0,4},{4,0},{8,12},{12,8},{16,20},{20,16},{24,28},{28,24},{1,5},{5... | collective-permute-start | bytes 1105928 | tf_op jit(solution)/shard_map/ppermute | solution.py:23
  42.0 0.0 collective-permute-start.9
  42.0 1.2 %collective-permute-done.9 = f32[8,128]{1,0:T(8,128)S(1)} collective-permute-done((f32[8,128]{1,0:T(8,128)S(1)}, f32[8,128]{1,0:T(8,128)S(1)}, u32[]{:S(2)}, u32[]{:S(2)}) %collective-permute-start.9) | collective-permute-done | bytes 4128 | tf_op jit(solution)/shard_map/ppermute | solution.py:23
  43.2 0.8 %collective-permute-start.10 = (f32[8,128]{1,0:T(8,128)S(1)}, f32[8,128]{1,0:T(8,128)S(1)}, u32[]{:S(2)}, u32[]{:S(2)}) collective-permute-start(f32[8,128]{1,0:T(8,128)S(1)} %add.30), channel_id=1, source_target_pairs={{0,2},{1,3},{2,0},{3,1},{4,6},{5,7},{6,4},{7,5},{8,10},{9,11},{10,... | collective-permute-start | bytes 12296 | tf_op jit(solution)/shard_map/ppermute | solution.py:23
  44.0 2.8 %collective-permute-done.10 = f32[8,128]{1,0:T(8,128)S(1)} collective-permute-done((f32[8,128]{1,0:T(8,128)S(1)}, f32[8,128]{1,0:T(8,128)S(1)}, u32[]{:S(2)}, u32[]{:S(2)}) %collective-permute-start.10) | collective-permute-done | bytes 4128 | tf_op jit(solution)/shard_map/ppermute | solution.py:23
  46.8 0.0 collective-permute-done.7.refs_2_
  46.8 0.7 %collective-permute-start.11 = (f32[8,128]{1,0:T(8,128)S(1)}, f32[8,128]{1,0:T(8,128)S(1)}, u32[]{:S(2)}, u32[]{:S(2)}) collective-permute-start(f32[8,128]{1,0:T(8,128)S(1)} %add.31), channel_id=1, source_target_pairs={{0,4},{4,0},{8,12},{12,8},{16,20},{20,16},{24,28},{28,24},{1,5},{5... | collective-permute-start | bytes 12296 | tf_op jit(solution)/shard_map/ppermute | solution.py:23
  47.5 0.8 %text_side_early.1.refs_1_ = f32[96,1152]{1,0:T(8,128)S(1)} custom-call(f32[1,2]{1,0:T(1,128)S(1)} %maximum_bitcast_fusion.settings, bf16[96,1152]{1,0:T(8,128)(2,1)S(1)} %slice.35.texts, bf16[104,1152]{1,0:T(8,128)(2,1)S(1)} %scorer.1.refs_0_, bf16[104,1152]{1,0:T(8,128)(2,1)S(1)} %collective-permute-done.2.refs_1_, ...), custom_call_target="tpu_custom_call" | custom-call | tf_op jit(solution)/shard_map/text_side_early/pallas_call | solution.py:138
  48.4 2.9 %collective-permute-done.11 = f32[8,128]{1,0:T(8,128)S(1)} collective-permute-done((f32[8,128]{1,0:T(8,128)S(1)}, f32[8,128]{1,0:T(8,128)S(1)}, u32[]{:S(2)}, u32[]{:S(2)}) %collective-permute-start.11) | collective-permute-done | bytes 4128 | tf_op jit(solution)/shard_map/ppermute | solution.py:23
  51.3 0.0 collective-permute-done.8.refs_3_.refs_0_
  51.3 0.5 text_side_mate.1
  51.8 1.4 %collective-permute-start.12 = (f32[112,1152]{1,0:T(8,128)S(1)}, f32[112,1152]{1,0:T(8,128)S(1)}, u32[]{:S(2)}, u32[]{:S(2)}) collective-permute-start(f32[112,1152]{1,0:T(8,128)S(1)} %pad_maximum_fusion), channel_id=1, source_target_pairs={{0,4},{4,0},{8,12},{12,8},{16,20},{20,16},{24,28},{28,24},{1,5},{5... | collective-permute-start | bytes 1548296 | tf_op jit(solution)/shard_map/ppermute | solution.py:23
  53.2 0.0 collective-permute-done.13
  53.2 0.1 slice_add_fusion.first
  53.3 1.8 %collective-permute-start.14 = (f32[8,128]{1,0:T(8,128)S(1)}, f32[8,128]{1,0:T(8,128)S(1)}, u32[]{:S(2)}, u32[]{:S(2)}) collective-permute-start(f32[8,128]{1,0:T(8,128)S(1)} %add.32), channel_id=1, source_target_pairs={{0,8},{4,12},{8,0},{12,4},{16,24},{20,28},{24,16},{28,20},{1,9},{5... | collective-permute-start | bytes 12296 | tf_op jit(solution)/shard_map/ppermute | solution.py:23
  55.1 1.1 %text_side_own.1.own_text = f32[96,1152]{1,0:T(8,128)S(1)} custom-call(f32[1,2]{1,0:T(1,128)S(1)} %maximum_bitcast_fusion.settings, bf16[96,1152]{1,0:T(8,128)(2,1)S(1)} %slice.26.own.texts, bf16[104,1152]{1,0:T(8,128)(2,1)S(1)} %scorer.1.refs_0_, bf16[104,1152]{1,0:T(8,128)(2,1)S(1)} %collective-permute-done.2.refs_1_, ...), custom_call_target="tpu_custom_call" | custom-call | tf_op jit(solution)/shard_map/text_side_own/pallas_call | solution.py:138
  56.2 0.7 %collective-permute-done.14 = f32[8,128]{1,0:T(8,128)S(1)} collective-permute-done((f32[8,128]{1,0:T(8,128)S(1)}, f32[8,128]{1,0:T(8,128)S(1)}, u32[]{:S(2)}, u32[]{:S(2)}) %collective-permute-start.14) | collective-permute-done | bytes 4128 | tf_op jit(solution)/shard_map/ppermute | solution.py:23
  57.0 1.2 %collective-permute-start.15 = (f32[8,128]{1,0:T(8,128)S(1)}, f32[8,128]{1,0:T(8,128)S(1)}, u32[]{:S(2)}, u32[]{:S(2)}) collective-permute-start(f32[8,128]{1,0:T(8,128)S(1)} %add.34), channel_id=1, source_target_pairs={{0,16},{4,20},{8,24},{12,28},{16,0},{20,4},{24,8},{28,12},{1,17},{... | collective-permute-start | bytes 12296 | tf_op jit(solution)/shard_map/ppermute | solution.py:23
  58.1 3.3 %collective-permute-done.15 = f32[8,128]{1,0:T(8,128)S(1)} collective-permute-done((f32[8,128]{1,0:T(8,128)S(1)}, f32[8,128]{1,0:T(8,128)S(1)}, u32[]{:S(2)}, u32[]{:S(2)}) %collective-permute-start.15) | collective-permute-done | bytes 4128 | tf_op jit(solution)/shard_map/ppermute | solution.py:23
  61.5 0.6 multiply_reduce_fusion
  62.1 2.6 %collective-permute-done.12.arrived = f32[112,1152]{1,0:T(8,128)S(1)} collective-permute-done((f32[112,1152]{1,0:T(8,128)S(1)}, f32[112,1152]{1,0:T(8,128)S(1)}, u32[]{:S(2)}, u32[]{:S(2)}) %collective-permute-start.12) | collective-permute-done | bytes 516128 | tf_op jit(solution)/shard_map/ppermute | solution.py:23
  64.7 1.0 %finish.1 = (f32[96,1152]{1,0:T(8,128)}, f32[96,1152]{1,0:T(8,128)}) custom-call(f32[96,1152]{1,0:T(8,128)S(1)} %text_side_own.1.own_text, f32[112,1152]{1,0:T(8,128)S(1)} %collective-permute-done.12.arrived, f32[80,1152]{1,0:T(8,128)S(1)} %slice_add_fusion.first, f32[16,1152]{1,0:T(8,128)S(1)} %slice.33.rest), custom_call_target="tpu_custom_call" | custom-call | tf_op jit(solution)/shard_map/finish/pallas_call | solution.py:138
  (15 shorter events, 0.2 us)
Async XLA Ops:
  0.6 8.6 %collective-permute-start = (bf16[96,1152]{1,0:T(8,128)(2,1)}, bf16[96,1152]{1,0:T(8,128)(2,1)S(1)}, u32[]{:S(2)}, u32[]{:S(2)}) collective-permute-start(bf16[96,1152]{1,0:T(8,128)(2,1)} %bitcast.14), channel_id=1, source_target_pairs={{0,2},{1,3},{2,0},{3,1},{4,6},{5,7},{6,4},{7,5},{8,10},{9,11},{10,... | collective-permute-start | bytes 663560 | tf_op jit(solution)/shard_map/ppermute | solution.py:23
  4.3 0.7 %copy-start.1 = (s32[1,96]{1,0:T(1,128)S(1)}, s32[1,96]{1,0:T(1,128)}, u32[]{:S(2)}) copy-start(s32[1,96]{1,0:T(1,128)} %param.8) | copy-start | bytes 1156
  6.2 3.1 %copy-start = (s32[4]{0:T(128)S(1)}, s32[4]{0:T(128)}, u32[]{:S(2)}) copy-start(s32[4]{0:T(128)} %param.9) | copy-start | bytes 52
  9.4 1.9 %collective-permute-start.1 = (bf16[96,1152]{1,0:T(8,128)(2,1)S(1)}, bf16[96,1152]{1,0:T(8,128)(2,1)S(1)}, u32[]{:S(2)}, u32[]{:S(2)}) collective-permute-start(bf16[96,1152]{1,0:T(8,128)(2,1)S(1)} %offer.1), channel_id=1, source_target_pairs={{0,1},{1,0},{2,3},{3,2},{4,5},{5,4},{6,7},{7,6},{8,9},{9,8},{10,11... | collective-permute-start | bytes 663560 | tf_op jit(solution)/shard_map/ppermute | solution.py:23
  9.5 16.3 %collective-permute-start.5 = (bf16[200,1152]{1,0:T(8,128)(2,1)S(1)}, bf16[200,1152]{1,0:T(8,128)(2,1)S(1)}, u32[]{:S(2)}, u32[]{:S(2)}) collective-permute-start(bf16[200,1152]{1,0:T(8,128)(2,1)S(1)} %pad_maximum_fusion.1), channel_id=1, source_target_pairs={{0,4},{4,0},{8,12},{12,8},{16,20},{20,16},{24,28},{28,24},{1,5},{5... | collective-permute-start | bytes 1382408 | tf_op jit(solution)/shard_map/ppermute | solution.py:23
  11.5 14.3 %collective-permute-start.4 = (bf16[96,1152]{1,0:T(8,128)(2,1)S(1)}, bf16[96,1152]{1,0:T(8,128)(2,1)S(1)}, u32[]{:S(2)}, u32[]{:S(2)}) collective-permute-start(bf16[96,1152]{1,0:T(8,128)(2,1)S(1)} %choose.1.refs_0_), channel_id=1, source_target_pairs={{0,8},{4,12},{8,0},{12,4},{16,24},{20,28},{24,16},{28,20},{1,9},{5... | collective-permute-start | bytes 663560 | tf_op jit(solution)/shard_map/ppermute | solution.py:23
  13.1 12.9 %collective-permute-start.3 = (bf16[96,1152]{1,0:T(8,128)(2,1)S(1)}, bf16[96,1152]{1,0:T(8,128)(2,1)S(1)}, u32[]{:S(2)}, u32[]{:S(2)}) collective-permute-start(bf16[96,1152]{1,0:T(8,128)(2,1)S(1)} %choose.1.refs_0_), channel_id=1, source_target_pairs={{0,16},{4,20},{8,24},{12,28},{16,0},{20,4},{24,8},{28,12},{1,17},{... | collective-permute-start | bytes 663560 | tf_op jit(solution)/shard_map/ppermute | solution.py:23
  25.4 14.1 %collective-permute-start.2 = (bf16[104,1152]{1,0:T(8,128)(2,1)S(1)}, bf16[104,1152]{1,0:T(8,128)(2,1)S(1)}, u32[]{:S(2)}, u32[]{:S(2)}) collective-permute-start(bf16[104,1152]{1,0:T(8,128)(2,1)S(1)} %scorer.1.refs_0_), channel_id=1, source_target_pairs={{0,16},{4,20},{8,24},{12,28},{16,0},{20,4},{24,8},{28,12},{1,17},{... | collective-permute-start | bytes 718856 | tf_op jit(solution)/shard_map/ppermute | solution.py:23
  26.0 10.2 %collective-permute-start.6 = (bf16[96,1152]{1,0:T(8,128)(2,1)S(1)}, bf16[96,1152]{1,0:T(8,128)(2,1)S(1)}, u32[]{:S(2)}, u32[]{:S(2)}) collective-permute-start(bf16[96,1152]{1,0:T(8,128)(2,1)S(1)} %collective-permute-done.3.refs_1_), channel_id=1, source_target_pairs={{0,8},{4,12},{8,0},{12,4},{16,24},{20,28},{24,16},{28,20},{1,9},{5... | collective-permute-start | bytes 663560 | tf_op jit(solution)/shard_map/ppermute | solution.py:23
  36.2 10.6 %collective-permute-start.7 = (bf16[104,1152]{1,0:T(8,128)(2,1)S(1)}, bf16[104,1152]{1,0:T(8,128)(2,1)S(1)}, u32[]{:S(2)}, u32[]{:S(2)}) collective-permute-start(bf16[104,1152]{1,0:T(8,128)(2,1)S(1)} %scorer.1.refs_0_), channel_id=1, source_target_pairs={{0,8},{4,12},{8,0},{12,4},{16,24},{20,28},{24,16},{28,20},{1,9},{5... | collective-permute-start | bytes 718856 | tf_op jit(solution)/shard_map/ppermute | solution.py:23
  39.5 11.8 %collective-permute-start.8 = (bf16[104,1152]{1,0:T(8,128)(2,1)S(1)}, bf16[104,1152]{1,0:T(8,128)(2,1)S(1)}, u32[]{:S(2)}, u32[]{:S(2)}) collective-permute-start(bf16[104,1152]{1,0:T(8,128)(2,1)S(1)} %collective-permute-done.2.refs_1_), channel_id=1, source_target_pairs={{0,8},{4,12},{8,0},{12,4},{16,24},{20,28},{24,16},{28,20},{1,9},{5... | collective-permute-start | bytes 718856 | tf_op jit(solution)/shard_map/ppermute | solution.py:23
  40.6 12.6 %collective-permute-start.13 = (f32[80,1152]{1,0:T(8,128)S(1)}, f32[80,1152]{1,0:T(8,128)S(1)}, u32[]{:S(2)}, u32[]{:S(2)}) collective-permute-start(f32[80,1152]{1,0:T(8,128)S(1)} %slice.32), channel_id=1, source_target_pairs={{0,4},{4,0},{8,12},{12,8},{16,20},{20,16},{24,28},{28,24},{1,5},{5... | collective-permute-start | bytes 1105928 | tf_op jit(solution)/shard_map/ppermute | solution.py:23
  42.0 1.2 %collective-permute-start.9 = (f32[8,128]{1,0:T(8,128)S(1)}, f32[8,128]{1,0:T(8,128)S(1)}, u32[]{:S(2)}, u32[]{:S(2)}) collective-permute-start(f32[8,128]{1,0:T(8,128)S(1)} %get-tuple-element.22), channel_id=1, source_target_pairs={{0,1},{1,0},{2,3},{3,2},{4,5},{5,4},{6,7},{7,6},{8,9},{9,8},{10,11... | collective-permute-start | bytes 12296 | tf_op jit(solution)/shard_map/ppermute | solution.py:23
  43.2 3.6 %collective-permute-start.10 = (f32[8,128]{1,0:T(8,128)S(1)}, f32[8,128]{1,0:T(8,128)S(1)}, u32[]{:S(2)}, u32[]{:S(2)}) collective-permute-start(f32[8,128]{1,0:T(8,128)S(1)} %add.30), channel_id=1, source_target_pairs={{0,2},{1,3},{2,0},{3,1},{4,6},{5,7},{6,4},{7,5},{8,10},{9,11},{10,... | collective-permute-start | bytes 12296 | tf_op jit(solution)/shard_map/ppermute | solution.py:23
  46.8 4.5 %collective-permute-start.11 = (f32[8,128]{1,0:T(8,128)S(1)}, f32[8,128]{1,0:T(8,128)S(1)}, u32[]{:S(2)}, u32[]{:S(2)}) collective-permute-start(f32[8,128]{1,0:T(8,128)S(1)} %add.31), channel_id=1, source_target_pairs={{0,4},{4,0},{8,12},{12,8},{16,20},{20,16},{24,28},{28,24},{1,5},{5... | collective-permute-start | bytes 12296 | tf_op jit(solution)/shard_map/ppermute | solution.py:23
  51.8 12.9 %collective-permute-start.12 = (f32[112,1152]{1,0:T(8,128)S(1)}, f32[112,1152]{1,0:T(8,128)S(1)}, u32[]{:S(2)}, u32[]{:S(2)}) collective-permute-start(f32[112,1152]{1,0:T(8,128)S(1)} %pad_maximum_fusion), channel_id=1, source_target_pairs={{0,4},{4,0},{8,12},{12,8},{16,20},{20,16},{24,28},{28,24},{1,5},{5... | collective-permute-start | bytes 1548296 | tf_op jit(solution)/shard_map/ppermute | solution.py:23
  53.3 3.7 %collective-permute-start.14 = (f32[8,128]{1,0:T(8,128)S(1)}, f32[8,128]{1,0:T(8,128)S(1)}, u32[]{:S(2)}, u32[]{:S(2)}) collective-permute-start(f32[8,128]{1,0:T(8,128)S(1)} %add.32), channel_id=1, source_target_pairs={{0,8},{4,12},{8,0},{12,4},{16,24},{20,28},{24,16},{28,20},{1,9},{5... | collective-permute-start | bytes 12296 | tf_op jit(solution)/shard_map/ppermute | solution.py:23
  57.0 4.5 %collective-permute-start.15 = (f32[8,128]{1,0:T(8,128)S(1)}, f32[8,128]{1,0:T(8,128)S(1)}, u32[]{:S(2)}, u32[]{:S(2)}) collective-permute-start(f32[8,128]{1,0:T(8,128)S(1)} %add.34), channel_id=1, source_target_pairs={{0,16},{4,20},{8,24},{12,28},{16,0},{20,4},{24,8},{28,12},{1,17},{... | collective-permute-start | bytes 12296 | tf_op jit(solution)/shard_map/ppermute | solution.py:23

commit v2 on v1

--- a/solution.py
+++ b/solution.py
@@ -195,7 +195,7 @@
         text_three_off = along(after(text_two_off, text_one_off, mate, scorer_image), 2)
         image_one_off = along(after(scorer_image, text_three_off), 2)
         image_two_off = along(scorer_image, 4)
-        column_texts = [partner_text, text_two_off, text_one_off, after(text_three_off, image_two_off)]
+        column_texts = [partner_text, text_two_off, text_one_off, text_three_off]
         grad_shape = texts.shape
         own_part, mate_part, total = call(
             image_kernel,
@@ -204,7 +204,7 @@
             "image_side",
             scratch=[(2 * rows, texts.shape[1]), (len(LINE) * rows, texts.shape[1])],
         )
-        image_three_off = along(image_two_off, 2)
+        image_three_off = along(after(image_two_off, own_part), 2)
         cut = rows * 5 // 6
         first_grads = own_part[:cut] + along(mate_part[:cut], 1)
         rest_own, rest = own_part[cut:], mate_part[cut:]

time: 65.9 us -> 64.5 us (0.979)
  waiting for transfers between devices: 27.4 us -> 24.7 us
  starting transfers between devices: 19.8 us -> 21 us
    ppermute x16, waiting for transfers between devices: 27.4 us -> 24.7 us  [exchange(): lax.ppermute(array, axis, [(place, mate(place)) for place in range(size)])]
    ppermute x16, starting transfers between devices: 19.8 us -> 21 us  [exchange(): lax.ppermute(array, axis, [(place, mate(place)) for place in range(size)])]
  transfers between devices with their start and end apart: 16 -> 16, of which waited for: 10 -> 9; matrix products, arithmetic and copies ran while one was open for 3% -> 3% of each run, Pallas kernels for 6% -> 6%
where the time goes in v2:
time: 64.5 us; the launch traced here: 64.3 us
  waiting for transfers between devices  24.7 us (38%)
  starting transfers between devices  21 us (33%)
  blocking collectives  9.52 us (15%)
  Pallas kernels  4.9 us (8%)
  between operations  2.11 us (3%)
  other arithmetic  1.89 us (3%)
    ppermute x16, waiting for transfers between devices, exchange(): lax.ppermute(array, axis, [(place, mate(place)) for place in range(size)])  24.7 us
    ppermute x16, starting transfers between devices, exchange(): lax.ppermute(array, axis, [(place, mate(place)) for place in range(size)])  21 us
    all_gather x1, blocking collectives, shards(): group_images = lax.all_gather(after(packed[:tailed], partner_text), 'group')  9.52 us
    pallas_call x8, Pallas kernels, call(): pl.pallas_call(kernel, out_shape=[jax.ShapeDtypeStruct(shape, dtype) for...  4.9 us
  transfers between devices with their start and end apart: 16, of which 9 were waited for; matrix products, arithmetic and copies ran while one was open for 3% of the time, Pallas kernels for 6%

profile of v2, /device:TPU:0, one launch (start us, length us, event | category | flops | bytes accessed | tf_op | source)
XLA Modules:
  0.0 64.3 jit_solution(820502413732826405)
XLA Ops:
  0.6 3.0 %collective-permute-start = (bf16[96,1152]{1,0:T(8,128)(2,1)}, bf16[96,1152]{1,0:T(8,128)(2,1)S(1)}, u32[]{:S(2)}, u32[]{:S(2)}) collective-permute-start(bf16[96,1152]{1,0:T(8,128)(2,1)} %bitcast.14), channel_id=1, source_target_pairs={{0,2},{1,3},{2,0},{3,1},{4,6},{5,7},{6,4},{7,5},{8,10},{9,11},{10,... | collective-permute-start | bytes 663560 | tf_op jit(solution)/shard_map/ppermute | solution.py:23
  4.3 0.0 copy-start.1
  5.0 0.0 copy-done.1
  5.0 0.1 maximum_bitcast_fusion.settings
  5.1 1.1 %pad_maximum_fusion.1 = bf16[200,1152]{1,0:T(8,128)(2,1)S(1)} fusion(bf16[96,1152]{1,0:T(8,128)(2,1)} %bitcast.15, bf16[8,1152]{1,0:T(8,128)(2,1)S(1)} %fusion.5, bf16[96,1152]{1,0:T(8,128)(2,1)} %bitcast.13), kind=kLoop, calls=%fused_computation.1 | loop fusion | flops 1382400 | bytes 921600 | tf_op jit(solution)/shard_map/concatenate | solution.py:174
  6.2 0.0 copy-start
  6.2 3.1 %collective-permute-done.across = bf16[96,1152]{1,0:T(8,128)(2,1)S(1)} collective-permute-done((bf16[96,1152]{1,0:T(8,128)(2,1)}, bf16[96,1152]{1,0:T(8,128)(2,1)S(1)}, u32[]{:S(2)}, u32[]{:S(2)}) %collective-permute-start) | collective-permute-done | bytes 221216 | tf_op jit(solution)/shard_map/ppermute | solution.py:23
  9.3 0.1 offer.1
  9.4 0.1 collective-permute-start.1
  9.5 1.8 %collective-permute-start.5 = (bf16[200,1152]{1,0:T(8,128)(2,1)S(1)}, bf16[200,1152]{1,0:T(8,128)(2,1)S(1)}, u32[]{:S(2)}, u32[]{:S(2)}) collective-permute-start(bf16[200,1152]{1,0:T(8,128)(2,1)S(1)} %pad_maximum_fusion.1), channel_id=1, source_target_pairs={{0,4},{4,0},{8,12},{12,8},{16,20},{20,16},{24,28},{28,24},{1,5},{5... | collective-permute-start | bytes 1382408 | tf_op jit(solution)/shard_map/ppermute | solution.py:23
  11.3 0.0 collective-permute-done.1.offered
  11.3 0.1 choose.1.refs_0_
  11.5 1.6 %collective-permute-start.4 = (bf16[96,1152]{1,0:T(8,128)(2,1)S(1)}, bf16[96,1152]{1,0:T(8,128)(2,1)S(1)}, u32[]{:S(2)}, u32[]{:S(2)}) collective-permute-start(bf16[96,1152]{1,0:T(8,128)(2,1)S(1)} %choose.1.refs_0_), channel_id=1, source_target_pairs={{0,8},{4,12},{8,0},{12,4},{16,24},{20,28},{24,16},{28,20},{1,9},{5... | collective-permute-start | bytes 663560 | tf_op jit(solution)/shard_map/ppermute | solution.py:23
  13.1 2.6 %collective-permute-start.3 = (bf16[96,1152]{1,0:T(8,128)(2,1)S(1)}, bf16[96,1152]{1,0:T(8,128)(2,1)S(1)}, u32[]{:S(2)}, u32[]{:S(2)}) collective-permute-start(bf16[96,1152]{1,0:T(8,128)(2,1)S(1)} %choose.1.refs_0_), channel_id=1, source_target_pairs={{0,16},{4,20},{8,24},{12,28},{16,0},{20,4},{24,8},{28,12},{1,17},{... | collective-permute-start | bytes 663560 | tf_op jit(solution)/shard_map/ppermute | solution.py:23
  15.7 9.5 %all-gather = bf16[416,1152]{1,0:T(8,128)(2,1)S(1)} all-gather(bf16[104,1152]{1,0:T(8,128)(2,1)S(1)} %slice.27.images), channel_id=2, replica_groups=mesh['blk'=8,'group'=4] {'group'}, dimensions={0}, use_global_device_ids=true | all-gather | bytes 1198080 | tf_op jit(solution)/shard_map/all_gather | solution.py:184
  25.2 0.2 scorer.1.refs_0_
  25.4 0.4 collective-permute-start.2
  25.8 0.0 collective-permute-done.5
  25.8 0.0 collective-permute-done.4.refs_2_
  25.8 0.2 collective-permute-done.3.refs_1_
  26.0 0.4 collective-permute-start.6
  26.5 9.7 %collective-permute-done.6.refs_3_ = bf16[96,1152]{1,0:T(8,128)(2,1)S(1)} collective-permute-done((bf16[96,1152]{1,0:T(8,128)(2,1)S(1)}, bf16[96,1152]{1,0:T(8,128)(2,1)S(1)}, u32[]{:S(2)}, u32[]{:S(2)}) %collective-permute-start.6) | collective-permute-done | bytes 221216 | tf_op jit(solution)/shard_map/ppermute | solution.py:23
  36.2 2.5 %collective-permute-start.7 = (bf16[104,1152]{1,0:T(8,128)(2,1)S(1)}, bf16[104,1152]{1,0:T(8,128)(2,1)S(1)}, u32[]{:S(2)}, u32[]{:S(2)}) collective-permute-start(bf16[104,1152]{1,0:T(8,128)(2,1)S(1)} %scorer.1.refs_0_), channel_id=1, source_target_pairs={{0,8},{4,12},{8,0},{12,4},{16,24},{20,28},{24,16},{28,20},{1,9},{5... | collective-permute-start | bytes 718856 | tf_op jit(solution)/shard_map/ppermute | solution.py:23
  38.7 1.0 %image_side.1 = (f32[96,1152]{1,0:T(8,128)S(1)}, f32[96,1152]{1,0:T(8,128)S(1)}, f32[8,128]{1,0:T(8,128)S(1)}) custom-call(f32[1,2]{1,0:T(1,128)S(1)} %maximum_bitcast_fusion.settings, bf16[104,1152]{1,0:T(8,128)(2,1)S(1)} %slice.27.images, bf16[104,1152]{1,0:T(8,128)(2,1)S(1)} %slice.34.mate, bf16[96,1152]{1,0:T(8,128)(2,1)S(1)} %choose.1.refs_0_, ...), custom_call_target="tpu_custom_call" | custom-call | tf_op jit(solution)/shard_map/image_side/pallas_call | solution.py:138
  39.7 0.0 collective-permute-done.2.refs_1_
  39.7 0.1 collective-permute-start.8
  39.9 1.4 %collective-permute-start.13 = (f32[80,1152]{1,0:T(8,128)S(1)}, f32[80,1152]{1,0:T(8,128)S(1)}, u32[]{:S(2)}, u32[]{:S(2)}) collective-permute-start(f32[80,1152]{1,0:T(8,128)S(1)} %slice.32), channel_id=1, source_target_pairs={{0,4},{4,0},{8,12},{12,8},{16,20},{20,16},{24,28},{28,24},{1,5},{5... | collective-permute-start | bytes 1105928 | tf_op jit(solution)/shard_map/ppermute | solution.py:23
  41.3 0.0 collective-permute-start.9
  41.3 1.2 %collective-permute-done.9 = f32[8,128]{1,0:T(8,128)S(1)} collective-permute-done((f32[8,128]{1,0:T(8,128)S(1)}, f32[8,128]{1,0:T(8,128)S(1)}, u32[]{:S(2)}, u32[]{:S(2)}) %collective-permute-start.9) | collective-permute-done | bytes 4128 | tf_op jit(solution)/shard_map/ppermute | solution.py:23
  42.5 0.8 %collective-permute-start.10 = (f32[8,128]{1,0:T(8,128)S(1)}, f32[8,128]{1,0:T(8,128)S(1)}, u32[]{:S(2)}, u32[]{:S(2)}) collective-permute-start(f32[8,128]{1,0:T(8,128)S(1)} %add.30), channel_id=1, source_target_pairs={{0,2},{1,3},{2,0},{3,1},{4,6},{5,7},{6,4},{7,5},{8,10},{9,11},{10,... | collective-permute-start | bytes 12296 | tf_op jit(solution)/shard_map/ppermute | solution.py:23
  43.3 2.8 %collective-permute-done.10 = f32[8,128]{1,0:T(8,128)S(1)} collective-permute-done((f32[8,128]{1,0:T(8,128)S(1)}, f32[8,128]{1,0:T(8,128)S(1)}, u32[]{:S(2)}, u32[]{:S(2)}) %collective-permute-start.10) | collective-permute-done | bytes 4128 | tf_op jit(solution)/shard_map/ppermute | solution.py:23
  46.1 0.0 collective-permute-done.7.refs_2_
  46.1 0.7 %collective-permute-start.11 = (f32[8,128]{1,0:T(8,128)S(1)}, f32[8,128]{1,0:T(8,128)S(1)}, u32[]{:S(2)}, u32[]{:S(2)}) collective-permute-start(f32[8,128]{1,0:T(8,128)S(1)} %add.31), channel_id=1, source_target_pairs={{0,4},{4,0},{8,12},{12,8},{16,20},{20,16},{24,28},{28,24},{1,5},{5... | collective-permute-start | bytes 12296 | tf_op jit(solution)/shard_map/ppermute | solution.py:23
  46.8 0.8 %text_side_early.1.refs_1_ = f32[96,1152]{1,0:T(8,128)S(1)} custom-call(f32[1,2]{1,0:T(1,128)S(1)} %maximum_bitcast_fusion.settings, bf16[96,1152]{1,0:T(8,128)(2,1)S(1)} %slice.35.texts, bf16[104,1152]{1,0:T(8,128)(2,1)S(1)} %scorer.1.refs_0_, bf16[104,1152]{1,0:T(8,128)(2,1)S(1)} %collective-permute-done.2.refs_1_, ...), custom_call_target="tpu_custom_call" | custom-call | tf_op jit(solution)/shard_map/text_side_early/pallas_call | solution.py:138
  47.6 2.6 %collective-permute-done.11 = f32[8,128]{1,0:T(8,128)S(1)} collective-permute-done((f32[8,128]{1,0:T(8,128)S(1)}, f32[8,128]{1,0:T(8,128)S(1)}, u32[]{:S(2)}, u32[]{:S(2)}) %collective-permute-start.11) | collective-permute-done | bytes 4128 | tf_op jit(solution)/shard_map/ppermute | solution.py:23
  50.2 0.0 collective-permute-done.8.refs_3_.refs_0_
  50.2 0.5 text_side_mate.1
  50.7 1.4 %collective-permute-start.12 = (f32[112,1152]{1,0:T(8,128)S(1)}, f32[112,1152]{1,0:T(8,128)S(1)}, u32[]{:S(2)}, u32[]{:S(2)}) collective-permute-start(f32[112,1152]{1,0:T(8,128)S(1)} %pad_maximum_fusion), channel_id=1, source_target_pairs={{0,4},{4,0},{8,12},{12,8},{16,20},{20,16},{24,28},{28,24},{1,5},{5... | collective-permute-start | bytes 1548296 | tf_op jit(solution)/shard_map/ppermute | solution.py:23
  52.2 0.0 collective-permute-done.13
  52.2 0.1 slice_add_fusion.first
  52.2 1.8 %collective-permute-start.14 = (f32[8,128]{1,0:T(8,128)S(1)}, f32[8,128]{1,0:T(8,128)S(1)}, u32[]{:S(2)}, u32[]{:S(2)}) collective-permute-start(f32[8,128]{1,0:T(8,128)S(1)} %add.32), channel_id=1, source_target_pairs={{0,8},{4,12},{8,0},{12,4},{16,24},{20,28},{24,16},{28,20},{1,9},{5... | collective-permute-start | bytes 12296 | tf_op jit(solution)/shard_map/ppermute | solution.py:23
  54.0 1.2 %text_side_own.1.own_text = f32[96,1152]{1,0:T(8,128)S(1)} custom-call(f32[1,2]{1,0:T(1,128)S(1)} %maximum_bitcast_fusion.settings, bf16[96,1152]{1,0:T(8,128)(2,1)S(1)} %slice.26.own.texts, bf16[104,1152]{1,0:T(8,128)(2,1)S(1)} %scorer.1.refs_0_, bf16[104,1152]{1,0:T(8,128)(2,1)S(1)} %collective-permute-done.2.refs_1_, ...), custom_call_target="tpu_custom_call" | custom-call | tf_op jit(solution)/shard_map/text_side_own/pallas_call | solution.py:138
  55.2 0.7 %collective-permute-done.14 = f32[8,128]{1,0:T(8,128)S(1)} collective-permute-done((f32[8,128]{1,0:T(8,128)S(1)}, f32[8,128]{1,0:T(8,128)S(1)}, u32[]{:S(2)}, u32[]{:S(2)}) %collective-permute-start.14) | collective-permute-done | bytes 4128 | tf_op jit(solution)/shard_map/ppermute | solution.py:23
  55.9 2.3 %collective-permute-start.15 = (f32[8,128]{1,0:T(8,128)S(1)}, f32[8,128]{1,0:T(8,128)S(1)}, u32[]{:S(2)}, u32[]{:S(2)}) collective-permute-start(f32[8,128]{1,0:T(8,128)S(1)} %add.34), channel_id=1, source_target_pairs={{0,16},{4,20},{8,24},{12,28},{16,0},{20,4},{24,8},{28,12},{1,17},{... | collective-permute-start | bytes 12296 | tf_op jit(solution)/shard_map/ppermute | solution.py:23
  58.2 2.2 %collective-permute-done.15 = f32[8,128]{1,0:T(8,128)S(1)} collective-permute-done((f32[8,128]{1,0:T(8,128)S(1)}, f32[8,128]{1,0:T(8,128)S(1)}, u32[]{:S(2)}, u32[]{:S(2)}) %collective-permute-start.15) | collective-permute-done | bytes 4128 | tf_op jit(solution)/shard_map/ppermute | solution.py:23
  60.4 0.6 multiply_reduce_fusion
  61.0 2.3 %collective-permute-done.12.arrived = f32[112,1152]{1,0:T(8,128)S(1)} collective-permute-done((f32[112,1152]{1,0:T(8,128)S(1)}, f32[112,1152]{1,0:T(8,128)S(1)}, u32[]{:S(2)}, u32[]{:S(2)}) %collective-permute-start.12) | collective-permute-done | bytes 516128 | tf_op jit(solution)/shard_map/ppermute | solution.py:23
  63.3 1.0 %finish.1 = (f32[96,1152]{1,0:T(8,128)}, f32[96,1152]{1,0:T(8,128)}) custom-call(f32[96,1152]{1,0:T(8,128)S(1)} %text_side_own.1.own_text, f32[112,1152]{1,0:T(8,128)S(1)} %collective-permute-done.12.arrived, f32[80,1152]{1,0:T(8,128)S(1)} %slice_add_fusion.first, f32[16,1152]{1,0:T(8,128)S(1)} %slice.33.rest), custom_call_target="tpu_custom_call" | custom-call | tf_op jit(solution)/shard_map/finish/pallas_call | solution.py:138
  (15 shorter events, 0.2 us)
Async XLA Ops:
  0.6 8.6 %collective-permute-start = (bf16[96,1152]{1,0:T(8,128)(2,1)}, bf16[96,1152]{1,0:T(8,128)(2,1)S(1)}, u32[]{:S(2)}, u32[]{:S(2)}) collective-permute-start(bf16[96,1152]{1,0:T(8,128)(2,1)} %bitcast.14), channel_id=1, source_target_pairs={{0,2},{1,3},{2,0},{3,1},{4,6},{5,7},{6,4},{7,5},{8,10},{9,11},{10,... | collective-permute-start | bytes 663560 | tf_op jit(solution)/shard_map/ppermute | solution.py:23
  4.3 0.7 %copy-start.1 = (s32[1,96]{1,0:T(1,128)S(1)}, s32[1,96]{1,0:T(1,128)}, u32[]{:S(2)}) copy-start(s32[1,96]{1,0:T(1,128)} %param.8) | copy-start | bytes 1156
  6.2 3.1 %copy-start = (s32[4]{0:T(128)S(1)}, s32[4]{0:T(128)}, u32[]{:S(2)}) copy-start(s32[4]{0:T(128)} %param.9) | copy-start | bytes 52
  9.4 1.9 %collective-permute-start.1 = (bf16[96,1152]{1,0:T(8,128)(2,1)S(1)}, bf16[96,1152]{1,0:T(8,128)(2,1)S(1)}, u32[]{:S(2)}, u32[]{:S(2)}) collective-permute-start(bf16[96,1152]{1,0:T(8,128)(2,1)S(1)} %offer.1), channel_id=1, source_target_pairs={{0,1},{1,0},{2,3},{3,2},{4,5},{5,4},{6,7},{7,6},{8,9},{9,8},{10,11... | collective-permute-start | bytes 663560 | tf_op jit(solution)/shard_map/ppermute | solution.py:23
  9.5 16.3 %collective-permute-start.5 = (bf16[200,1152]{1,0:T(8,128)(2,1)S(1)}, bf16[200,1152]{1,0:T(8,128)(2,1)S(1)}, u32[]{:S(2)}, u32[]{:S(2)}) collective-permute-start(bf16[200,1152]{1,0:T(8,128)(2,1)S(1)} %pad_maximum_fusion.1), channel_id=1, source_target_pairs={{0,4},{4,0},{8,12},{12,8},{16,20},{20,16},{24,28},{28,24},{1,5},{5... | collective-permute-start | bytes 1382408 | tf_op jit(solution)/shard_map/ppermute | solution.py:23
  11.5 14.3 %collective-permute-start.4 = (bf16[96,1152]{1,0:T(8,128)(2,1)S(1)}, bf16[96,1152]{1,0:T(8,128)(2,1)S(1)}, u32[]{:S(2)}, u32[]{:S(2)}) collective-permute-start(bf16[96,1152]{1,0:T(8,128)(2,1)S(1)} %choose.1.refs_0_), channel_id=1, source_target_pairs={{0,8},{4,12},{8,0},{12,4},{16,24},{20,28},{24,16},{28,20},{1,9},{5... | collective-permute-start | bytes 663560 | tf_op jit(solution)/shard_map/ppermute | solution.py:23
  13.1 12.9 %collective-permute-start.3 = (bf16[96,1152]{1,0:T(8,128)(2,1)S(1)}, bf16[96,1152]{1,0:T(8,128)(2,1)S(1)}, u32[]{:S(2)}, u32[]{:S(2)}) collective-permute-start(bf16[96,1152]{1,0:T(8,128)(2,1)S(1)} %choose.1.refs_0_), channel_id=1, source_target_pairs={{0,16},{4,20},{8,24},{12,28},{16,0},{20,4},{24,8},{28,12},{1,17},{... | collective-permute-start | bytes 663560 | tf_op jit(solution)/shard_map/ppermute | solution.py:23
  25.4 14.3 %collective-permute-start.2 = (bf16[104,1152]{1,0:T(8,128)(2,1)S(1)}, bf16[104,1152]{1,0:T(8,128)(2,1)S(1)}, u32[]{:S(2)}, u32[]{:S(2)}) collective-permute-start(bf16[104,1152]{1,0:T(8,128)(2,1)S(1)} %scorer.1.refs_0_), channel_id=1, source_target_pairs={{0,16},{4,20},{8,24},{12,28},{16,0},{20,4},{24,8},{28,12},{1,17},{... | collective-permute-start | bytes 718856 | tf_op jit(solution)/shard_map/ppermute | solution.py:23
  26.0 10.2 %collective-permute-start.6 = (bf16[96,1152]{1,0:T(8,128)(2,1)S(1)}, bf16[96,1152]{1,0:T(8,128)(2,1)S(1)}, u32[]{:S(2)}, u32[]{:S(2)}) collective-permute-start(bf16[96,1152]{1,0:T(8,128)(2,1)S(1)} %collective-permute-done.3.refs_1_), channel_id=1, source_target_pairs={{0,8},{4,12},{8,0},{12,4},{16,24},{20,28},{24,16},{28,20},{1,9},{5... | collective-permute-start | bytes 663560 | tf_op jit(solution)/shard_map/ppermute | solution.py:23
  36.2 9.9 %collective-permute-start.7 = (bf16[104,1152]{1,0:T(8,128)(2,1)S(1)}, bf16[104,1152]{1,0:T(8,128)(2,1)S(1)}, u32[]{:S(2)}, u32[]{:S(2)}) collective-permute-start(bf16[104,1152]{1,0:T(8,128)(2,1)S(1)} %scorer.1.refs_0_), channel_id=1, source_target_pairs={{0,8},{4,12},{8,0},{12,4},{16,24},{20,28},{24,16},{28,20},{1,9},{5... | collective-permute-start | bytes 718856 | tf_op jit(solution)/shard_map/ppermute | solution.py:23
  39.7 10.5 %collective-permute-start.8 = (bf16[104,1152]{1,0:T(8,128)(2,1)S(1)}, bf16[104,1152]{1,0:T(8,128)(2,1)S(1)}, u32[]{:S(2)}, u32[]{:S(2)}) collective-permute-start(bf16[104,1152]{1,0:T(8,128)(2,1)S(1)} %collective-permute-done.2.refs_1_), channel_id=1, source_target_pairs={{0,8},{4,12},{8,0},{12,4},{16,24},{20,28},{24,16},{28,20},{1,9},{5... | collective-permute-start | bytes 718856 | tf_op jit(solution)/shard_map/ppermute | solution.py:23
  39.9 12.3 %collective-permute-start.13 = (f32[80,1152]{1,0:T(8,128)S(1)}, f32[80,1152]{1,0:T(8,128)S(1)}, u32[]{:S(2)}, u32[]{:S(2)}) collective-permute-start(f32[80,1152]{1,0:T(8,128)S(1)} %slice.32), channel_id=1, source_target_pairs={{0,4},{4,0},{8,12},{12,8},{16,20},{20,16},{24,28},{28,24},{1,5},{5... | collective-permute-start | bytes 1105928 | tf_op jit(solution)/shard_map/ppermute | solution.py:23
  41.3 1.2 %collective-permute-start.9 = (f32[8,128]{1,0:T(8,128)S(1)}, f32[8,128]{1,0:T(8,128)S(1)}, u32[]{:S(2)}, u32[]{:S(2)}) collective-permute-start(f32[8,128]{1,0:T(8,128)S(1)} %get-tuple-element.23), channel_id=1, source_target_pairs={{0,1},{1,0},{2,3},{3,2},{4,5},{5,4},{6,7},{7,6},{8,9},{9,8},{10,11... | collective-permute-start | bytes 12296 | tf_op jit(solution)/shard_map/ppermute | solution.py:23
  42.5 3.6 %collective-permute-start.10 = (f32[8,128]{1,0:T(8,128)S(1)}, f32[8,128]{1,0:T(8,128)S(1)}, u32[]{:S(2)}, u32[]{:S(2)}) collective-permute-start(f32[8,128]{1,0:T(8,128)S(1)} %add.30), channel_id=1, source_target_pairs={{0,2},{1,3},{2,0},{3,1},{4,6},{5,7},{6,4},{7,5},{8,10},{9,11},{10,... | collective-permute-start | bytes 12296 | tf_op jit(solution)/shard_map/ppermute | solution.py:23
  46.1 4.1 %collective-permute-start.11 = (f32[8,128]{1,0:T(8,128)S(1)}, f32[8,128]{1,0:T(8,128)S(1)}, u32[]{:S(2)}, u32[]{:S(2)}) collective-permute-start(f32[8,128]{1,0:T(8,128)S(1)} %add.31), channel_id=1, source_target_pairs={{0,4},{4,0},{8,12},{12,8},{16,20},{20,16},{24,28},{28,24},{1,5},{5... | collective-permute-start | bytes 12296 | tf_op jit(solution)/shard_map/ppermute | solution.py:23
  50.7 12.6 %collective-permute-start.12 = (f32[112,1152]{1,0:T(8,128)S(1)}, f32[112,1152]{1,0:T(8,128)S(1)}, u32[]{:S(2)}, u32[]{:S(2)}) collective-permute-start(f32[112,1152]{1,0:T(8,128)S(1)} %pad_maximum_fusion), channel_id=1, source_target_pairs={{0,4},{4,0},{8,12},{12,8},{16,20},{20,16},{24,28},{28,24},{1,5},{5... | collective-permute-start | bytes 1548296 | tf_op jit(solution)/shard_map/ppermute | solution.py:23
  52.2 3.7 %collective-permute-start.14 = (f32[8,128]{1,0:T(8,128)S(1)}, f32[8,128]{1,0:T(8,128)S(1)}, u32[]{:S(2)}, u32[]{:S(2)}) collective-permute-start(f32[8,128]{1,0:T(8,128)S(1)} %add.32), channel_id=1, source_target_pairs={{0,8},{4,12},{8,0},{12,4},{16,24},{20,28},{24,16},{28,20},{1,9},{5... | collective-permute-start | bytes 12296 | tf_op jit(solution)/shard_map/ppermute | solution.py:23
  55.9 4.5 %collective-permute-start.15 = (f32[8,128]{1,0:T(8,128)S(1)}, f32[8,128]{1,0:T(8,128)S(1)}, u32[]{:S(2)}, u32[]{:S(2)}) collective-permute-start(f32[8,128]{1,0:T(8,128)S(1)} %add.34), channel_id=1, source_target_pairs={{0,16},{4,20},{8,24},{12,28},{16,0},{20,4},{24,8},{28,12},{1,17},{... | collective-permute-start | bytes 12296 | tf_op jit(solution)/shard_map/ppermute | solution.py:23

commit v3 on v2

--- a/solution.py
+++ b/solution.py
@@ -127,11 +127,11 @@
     part[...] = temper * total + earlier[0][...] if earlier else temper * total
 
 
-def finish_kernel(own_text, arrived, first, rest, text_grads, image_grads):
-    rows, cut = own_text.shape[0], first.shape[0]
-    text_grads[...] = own_text[...] + arrived[:rows]
+def finish_kernel(own_text, text_part, first, rest_own, rest, text_grads, image_grads):
+    cut = first.shape[0]
+    text_grads[...] = own_text[...] + text_part[...]
     image_grads[:cut] = first[...]
-    image_grads[cut:] = rest[...] + arrived[rows:]
+    image_grads[cut:] = rest_own[...] + rest[...]
 
 
 def call(kernel, arrays, shapes, name, dtype=jnp.float32, scratch=()):
@@ -212,15 +212,16 @@
         total = hop_sum(after(total, image_one_off), hops[2:3])
         early_images = [scorer_image, image_two_off, image_one_off]
         early_part = call(functools.partial(text_kernel, 1, 3), [settings, mate[tailed:], *early_images], [grad_shape], "text_side_early")[0]
-        last_image = after(image_three_off, total, early_part)
+        rest = along(after(rest, early_part), 1)
+        last_image = after(image_three_off, total)
         mate_part = call(functools.partial(text_kernel, 1, 1), [settings, mate[tailed:], last_image, early_part], [grad_shape], "text_side_mate")[0]
         column_images = early_images + [last_image]
-        arrived = along(jnp.concatenate([mate_part, rest]), 1)
+        text_part = along(mate_part, 1)
         own_part = call(functools.partial(text_kernel, 0, 4), [settings, own_texts, *column_images], [grad_shape], "text_side_own")[0]
         text_grads, image_grads = call(
-            finish_kernel, [own_part, arrived, first_grads, rest_own], [grad_shape, grad_shape], "finish"
+            finish_kernel, [own_part, text_part, first_grads, rest_own, rest], [grad_shape, grad_shape], "finish"
         )
-        total = after(hop_sum(after(total, first_grads), hops[3:4]), own_part)
+        total = after(hop_sum(after(total, first_grads, rest), hops[3:4]), own_part)
         hops = hops[4:]
     else:
         temper = jnp.exp(log_temp[0])

time: 64.5 us -> 64.9 us (level)
  waiting for transfers between devices: 24.7 us -> 25.8 us
    ppermute x16 -> x17, waiting for transfers between devices: 24.7 us -> 25.8 us  [exchange(): lax.ppermute(array, axis, [(place, mate(place)) for place in range(size)])]
    ppermute x16 -> x17, starting transfers between devices: 21 us -> 20.4 us  [exchange(): lax.ppermute(array, axis, [(place, mate(place)) for place in range(size)])]
  transfers between devices with their start and end apart: 16 -> 17, of which waited for: 9 -> 11; matrix products, arithmetic and copies ran while one was open for 3% -> 3% of each run, Pallas kernels for 6% -> 6%
where the time goes in v3:
time: 64.9 us; the launch traced here: 64.7 us
  waiting for transfers between devices  25.8 us (40%)
  starting transfers between devices  20.4 us (31%)
  blocking collectives  9.52 us (15%)
  Pallas kernels  4.9 us (8%)
  between operations  2.1 us (3%)
  other arithmetic  1.85 us (3%)
    ppermute x17, waiting for transfers between devices, exchange(): lax.ppermute(array, axis, [(place, mate(place)) for place in range(size)])  25.8 us
    ppermute x17, starting transfers between devices, exchange(): lax.ppermute(array, axis, [(place, mate(place)) for place in range(size)])  20.4 us
    all_gather x1, blocking collectives, shards(): group_images = lax.all_gather(after(packed[:tailed], partner_text), 'group')  9.52 us
    pallas_call x8, Pallas kernels, call(): pl.pallas_call(kernel, out_shape=[jax.ShapeDtypeStruct(shape, dtype) for...  4.9 us
  transfers between devices with their start and end apart: 17, of which 11 were waited for; matrix products, arithmetic and copies ran while one was open for 3% of the time, Pallas kernels for 6%

profile of v3, /device:TPU:0, one launch (start us, length us, event | category | flops | bytes accessed | tf_op | source)
XLA Modules:
  0.0 64.7 jit_solution(5646853201469662064)
XLA Ops:
  0.6 3.0 %collective-permute-start = (bf16[96,1152]{1,0:T(8,128)(2,1)}, bf16[96,1152]{1,0:T(8,128)(2,1)S(1)}, u32[]{:S(2)}, u32[]{:S(2)}) collective-permute-start(bf16[96,1152]{1,0:T(8,128)(2,1)} %bitcast.14), channel_id=1, source_target_pairs={{0,2},{1,3},{2,0},{3,1},{4,6},{5,7},{6,4},{7,5},{8,10},{9,11},{10,... | collective-permute-start | bytes 663560 | tf_op jit(solution)/shard_map/ppermute | solution.py:23
  5.0 0.1 maximum_bitcast_fusion.settings
  5.1 1.1 %pad_maximum_fusion = bf16[200,1152]{1,0:T(8,128)(2,1)S(1)} fusion(bf16[96,1152]{1,0:T(8,128)(2,1)} %bitcast.15, bf16[8,1152]{1,0:T(8,128)(2,1)S(1)} %fusion.5, bf16[96,1152]{1,0:T(8,128)(2,1)} %bitcast.13), kind=kLoop, calls=%fused_computation | loop fusion | flops 1382400 | bytes 921600 | tf_op jit(solution)/shard_map/concatenate | solution.py:174
  6.2 0.0 copy-start
  6.2 3.1 %collective-permute-done.across = bf16[96,1152]{1,0:T(8,128)(2,1)S(1)} collective-permute-done((bf16[96,1152]{1,0:T(8,128)(2,1)}, bf16[96,1152]{1,0:T(8,128)(2,1)S(1)}, u32[]{:S(2)}, u32[]{:S(2)}) %collective-permute-start) | collective-permute-done | bytes 221216 | tf_op jit(solution)/shard_map/ppermute | solution.py:23
  9.3 0.1 offer.1
  9.4 0.1 collective-permute-start.1
  9.5 1.8 %collective-permute-start.5 = (bf16[200,1152]{1,0:T(8,128)(2,1)S(1)}, bf16[200,1152]{1,0:T(8,128)(2,1)S(1)}, u32[]{:S(2)}, u32[]{:S(2)}) collective-permute-start(bf16[200,1152]{1,0:T(8,128)(2,1)S(1)} %pad_maximum_fusion), channel_id=1, source_target_pairs={{0,4},{4,0},{8,12},{12,8},{16,20},{20,16},{24,28},{28,24},{1,5},{5... | collective-permute-start | bytes 1382408 | tf_op jit(solution)/shard_map/ppermute | solution.py:23
  11.3 0.0 collective-permute-done.1.offered
  11.3 0.1 choose.1.refs_0_
  11.5 1.6 %collective-permute-start.4 = (bf16[96,1152]{1,0:T(8,128)(2,1)S(1)}, bf16[96,1152]{1,0:T(8,128)(2,1)S(1)}, u32[]{:S(2)}, u32[]{:S(2)}) collective-permute-start(bf16[96,1152]{1,0:T(8,128)(2,1)S(1)} %choose.1.refs_0_), channel_id=1, source_target_pairs={{0,8},{4,12},{8,0},{12,4},{16,24},{20,28},{24,16},{28,20},{1,9},{5... | collective-permute-start | bytes 663560 | tf_op jit(solution)/shard_map/ppermute | solution.py:23
  13.1 2.6 %collective-permute-start.3 = (bf16[96,1152]{1,0:T(8,128)(2,1)S(1)}, bf16[96,1152]{1,0:T(8,128)(2,1)S(1)}, u32[]{:S(2)}, u32[]{:S(2)}) collective-permute-start(bf16[96,1152]{1,0:T(8,128)(2,1)S(1)} %choose.1.refs_0_), channel_id=1, source_target_pairs={{0,16},{4,20},{8,24},{12,28},{16,0},{20,4},{24,8},{28,12},{1,17},{... | collective-permute-start | bytes 663560 | tf_op jit(solution)/shard_map/ppermute | solution.py:23
  15.7 9.5 %all-gather = bf16[416,1152]{1,0:T(8,128)(2,1)S(1)} all-gather(bf16[104,1152]{1,0:T(8,128)(2,1)S(1)} %slice.27.images), channel_id=2, replica_groups=mesh['blk'=8,'group'=4] {'group'}, dimensions={0}, use_global_device_ids=true | all-gather | bytes 1198080 | tf_op jit(solution)/shard_map/all_gather | solution.py:184
  25.2 0.2 scorer.1.refs_0_
  25.4 0.0 collective-permute-done.5
  25.4 0.0 collective-permute-done.4.refs_2_
  25.4 0.6 collective-permute-done.3.refs_1_
  26.0 0.4 collective-permute-start.6
  26.5 2.6 %collective-permute-start.2 = (bf16[104,1152]{1,0:T(8,128)(2,1)S(1)}, bf16[104,1152]{1,0:T(8,128)(2,1)S(1)}, u32[]{:S(2)}, u32[]{:S(2)}) collective-permute-start(bf16[104,1152]{1,0:T(8,128)(2,1)S(1)} %scorer.1.refs_0_), channel_id=1, source_target_pairs={{0,16},{4,20},{8,24},{12,28},{16,0},{20,4},{24,8},{28,12},{1,17},{... | collective-permute-start | bytes 718856 | tf_op jit(solution)/shard_map/ppermute | solution.py:23
  29.1 7.8 %collective-permute-done.6.refs_3_ = bf16[96,1152]{1,0:T(8,128)(2,1)S(1)} collective-permute-done((bf16[96,1152]{1,0:T(8,128)(2,1)S(1)}, bf16[96,1152]{1,0:T(8,128)(2,1)S(1)}, u32[]{:S(2)}, u32[]{:S(2)}) %collective-permute-start.6) | collective-permute-done | bytes 221216 | tf_op jit(solution)/shard_map/ppermute | solution.py:23
  36.9 1.0 %image_side.1 = (f32[96,1152]{1,0:T(8,128)S(1)}, f32[96,1152]{1,0:T(8,128)S(1)}, f32[8,128]{1,0:T(8,128)S(1)}) custom-call(f32[1,2]{1,0:T(1,128)S(1)} %maximum_bitcast_fusion.settings, bf16[104,1152]{1,0:T(8,128)(2,1)S(1)} %slice.27.images, bf16[104,1152]{1,0:T(8,128)(2,1)S(1)} %slice.34.mate, bf16[96,1152]{1,0:T(8,128)(2,1)S(1)} %choose.1.refs_0_, ...), custom_call_target="tpu_custom_call" | custom-call | tf_op jit(solution)/shard_map/image_side/pallas_call | solution.py:138
  38.0 1.4 %collective-permute-start.13 = (f32[80,1152]{1,0:T(8,128)S(1)}, f32[80,1152]{1,0:T(8,128)S(1)}, u32[]{:S(2)}, u32[]{:S(2)}) collective-permute-start(f32[80,1152]{1,0:T(8,128)S(1)} %slice.31), channel_id=1, source_target_pairs={{0,4},{4,0},{8,12},{12,8},{16,20},{20,16},{24,28},{28,24},{1,5},{5... | collective-permute-start | bytes 1105928 | tf_op jit(solution)/shard_map/ppermute | solution.py:23
  39.3 0.0 collective-permute-start.7
  39.3 0.5 collective-permute-done.2.refs_1_
  39.8 1.6 %collective-permute-start.8 = (bf16[104,1152]{1,0:T(8,128)(2,1)S(1)}, bf16[104,1152]{1,0:T(8,128)(2,1)S(1)}, u32[]{:S(2)}, u32[]{:S(2)}) collective-permute-start(bf16[104,1152]{1,0:T(8,128)(2,1)S(1)} %collective-permute-done.2.refs_1_), channel_id=1, source_target_pairs={{0,8},{4,12},{8,0},{12,4},{16,24},{20,28},{24,16},{28,20},{1,9},{5... | collective-permute-start | bytes 718856 | tf_op jit(solution)/shard_map/ppermute | solution.py:23
  41.4 0.0 collective-permute-start.9
  41.4 1.2 %collective-permute-done.9 = f32[8,128]{1,0:T(8,128)S(1)} collective-permute-done((f32[8,128]{1,0:T(8,128)S(1)}, f32[8,128]{1,0:T(8,128)S(1)}, u32[]{:S(2)}, u32[]{:S(2)}) %collective-permute-start.9) | collective-permute-done | bytes 4128 | tf_op jit(solution)/shard_map/ppermute | solution.py:23
  42.5 1.4 %collective-permute-start.10 = (f32[8,128]{1,0:T(8,128)S(1)}, f32[8,128]{1,0:T(8,128)S(1)}, u32[]{:S(2)}, u32[]{:S(2)}) collective-permute-start(f32[8,128]{1,0:T(8,128)S(1)} %add.30), channel_id=1, source_target_pairs={{0,2},{1,3},{2,0},{3,1},{4,6},{5,7},{6,4},{7,5},{8,10},{9,11},{10,... | collective-permute-start | bytes 12296 | tf_op jit(solution)/shard_map/ppermute | solution.py:23
  44.0 2.2 %collective-permute-done.10 = f32[8,128]{1,0:T(8,128)S(1)} collective-permute-done((f32[8,128]{1,0:T(8,128)S(1)}, f32[8,128]{1,0:T(8,128)S(1)}, u32[]{:S(2)}, u32[]{:S(2)}) %collective-permute-start.10) | collective-permute-done | bytes 4128 | tf_op jit(solution)/shard_map/ppermute | solution.py:23
  46.2 1.9 %collective-permute-done.7.refs_2_ = bf16[104,1152]{1,0:T(8,128)(2,1)S(1)} collective-permute-done((bf16[104,1152]{1,0:T(8,128)(2,1)S(1)}, bf16[104,1152]{1,0:T(8,128)(2,1)S(1)}, u32[]{:S(2)}, u32[]{:S(2)}) %collective-permute-start.7) | collective-permute-done | bytes 239648 | tf_op jit(solution)/shard_map/ppermute | solution.py:23
  48.1 0.7 %collective-permute-start.11 = (f32[8,128]{1,0:T(8,128)S(1)}, f32[8,128]{1,0:T(8,128)S(1)}, u32[]{:S(2)}, u32[]{:S(2)}) collective-permute-start(f32[8,128]{1,0:T(8,128)S(1)} %add.31), channel_id=1, source_target_pairs={{0,4},{4,0},{8,12},{12,8},{16,20},{20,16},{24,28},{28,24},{1,5},{5... | collective-permute-start | bytes 12296 | tf_op jit(solution)/shard_map/ppermute | solution.py:23
  48.9 0.8 %text_side_early.1.refs_1_ = f32[96,1152]{1,0:T(8,128)S(1)} custom-call(f32[1,2]{1,0:T(1,128)S(1)} %maximum_bitcast_fusion.settings, bf16[96,1152]{1,0:T(8,128)(2,1)S(1)} %slice.35.texts, bf16[104,1152]{1,0:T(8,128)(2,1)S(1)} %scorer.1.refs_0_, bf16[104,1152]{1,0:T(8,128)(2,1)S(1)} %collective-permute-done.2.refs_1_, ...), custom_call_target="tpu_custom_call" | custom-call | tf_op jit(solution)/shard_map/text_side_early/pallas_call | solution.py:138
  49.7 1.4 %collective-permute-start.14 = (f32[16,1152]{1,0:T(8,128)S(1)}, f32[16,1152]{1,0:T(8,128)S(1)}, u32[]{:S(2)}, u32[]{:S(2)}) collective-permute-start(f32[16,1152]{1,0:T(8,128)S(1)} %slice.33), channel_id=1, source_target_pairs={{0,4},{4,0},{8,12},{12,8},{16,20},{20,16},{24,28},{28,24},{1,5},{5... | collective-permute-start | bytes 221192 | tf_op jit(solution)/shard_map/ppermute | solution.py:23
  51.1 0.6 collective-permute-done.11
  51.7 0.0 collective-permute-done.8.refs_3_.refs_0_
  51.7 0.5 text_side_mate.1
  52.2 0.8 %collective-permute-start.12 = (f32[96,1152]{1,0:T(8,128)S(1)}, f32[96,1152]{1,0:T(8,128)S(1)}, u32[]{:S(2)}, u32[]{:S(2)}) collective-permute-start(f32[96,1152]{1,0:T(8,128)S(1)} %text_side_mate.1), channel_id=1, source_target_pairs={{0,4},{4,0},{8,12},{12,8},{16,20},{20,16},{24,28},{28,24},{1,5},{5... | collective-permute-start | bytes 1327112 | tf_op jit(solution)/shard_map/ppermute | solution.py:23
  53.0 0.0 collective-permute-done.13
  53.0 0.1 slice_add_fusion.first
  53.0 1.9 %collective-permute-done.14.rest = f32[16,1152]{1,0:T(8,128)S(1)} collective-permute-done((f32[16,1152]{1,0:T(8,128)S(1)}, f32[16,1152]{1,0:T(8,128)S(1)}, u32[]{:S(2)}, u32[]{:S(2)}) %collective-permute-start.14) | collective-permute-done | bytes 73760 | tf_op jit(solution)/shard_map/ppermute | solution.py:23
  55.0 0.0 collective-permute-start.15
  55.0 1.1 %text_side_own.1.own_text = f32[96,1152]{1,0:T(8,128)S(1)} custom-call(f32[1,2]{1,0:T(1,128)S(1)} %maximum_bitcast_fusion.settings, bf16[96,1152]{1,0:T(8,128)(2,1)S(1)} %slice.26.own.texts, bf16[104,1152]{1,0:T(8,128)(2,1)S(1)} %scorer.1.refs_0_, bf16[104,1152]{1,0:T(8,128)(2,1)S(1)} %collective-permute-done.2.refs_1_, ...), custom_call_target="tpu_custom_call" | custom-call | tf_op jit(solution)/shard_map/text_side_own/pallas_call | solution.py:138
  56.1 2.5 %collective-permute-done.15 = f32[8,128]{1,0:T(8,128)S(1)} collective-permute-done((f32[8,128]{1,0:T(8,128)S(1)}, f32[8,128]{1,0:T(8,128)S(1)}, u32[]{:S(2)}, u32[]{:S(2)}) %collective-permute-start.15) | collective-permute-done | bytes 4128 | tf_op jit(solution)/shard_map/ppermute | solution.py:23
  58.6 1.0 %collective-permute-start.16 = (f32[8,128]{1,0:T(8,128)S(1)}, f32[8,128]{1,0:T(8,128)S(1)}, u32[]{:S(2)}, u32[]{:S(2)}) collective-permute-start(f32[8,128]{1,0:T(8,128)S(1)} %add.34), channel_id=1, source_target_pairs={{0,16},{4,20},{8,24},{12,28},{16,0},{20,4},{24,8},{28,12},{1,17},{... | collective-permute-start | bytes 12296 | tf_op jit(solution)/shard_map/ppermute | solution.py:23
  59.5 3.5 %collective-permute-done.16 = f32[8,128]{1,0:T(8,128)S(1)} collective-permute-done((f32[8,128]{1,0:T(8,128)S(1)}, f32[8,128]{1,0:T(8,128)S(1)}, u32[]{:S(2)}, u32[]{:S(2)}) %collective-permute-start.16) | collective-permute-done | bytes 4128 | tf_op jit(solution)/shard_map/ppermute | solution.py:23
  63.1 0.6 multiply_reduce_fusion
  63.7 0.0 collective-permute-done.12.text_part
  63.7 1.0 %finish.1 = (f32[96,1152]{1,0:T(8,128)}, f32[96,1152]{1,0:T(8,128)}) custom-call(f32[96,1152]{1,0:T(8,128)S(1)} %text_side_own.1.own_text, f32[96,1152]{1,0:T(8,128)S(1)} %collective-permute-done.12.text_part, f32[80,1152]{1,0:T(8,128)S(1)} %slice_add_fusion.first, f32[16,1152]{1,0:T(8,128)S(1)} %slice.32.rest_own, f32[16,1152]{1,0:T(8,128)S(1)} %collective-permute-done.14.rest), custom_call_target="tpu_custom_call" | custom-call | tf_op jit(solution)/shard_map/finish/pallas_call | solution.py:138
  (16 shorter events, 0.2 us)
Async XLA Ops:
  0.6 8.6 %collective-permute-start = (bf16[96,1152]{1,0:T(8,128)(2,1)}, bf16[96,1152]{1,0:T(8,128)(2,1)S(1)}, u32[]{:S(2)}, u32[]{:S(2)}) collective-permute-start(bf16[96,1152]{1,0:T(8,128)(2,1)} %bitcast.14), channel_id=1, source_target_pairs={{0,2},{1,3},{2,0},{3,1},{4,6},{5,7},{6,4},{7,5},{8,10},{9,11},{10,... | collective-permute-start | bytes 663560 | tf_op jit(solution)/shard_map/ppermute | solution.py:23
  4.3 0.7 %copy-start.1 = (s32[1,96]{1,0:T(1,128)S(1)}, s32[1,96]{1,0:T(1,128)}, u32[]{:S(2)}) copy-start(s32[1,96]{1,0:T(1,128)} %param.8) | copy-start | bytes 1156
  6.2 3.1 %copy-start = (s32[4]{0:T(128)S(1)}, s32[4]{0:T(128)}, u32[]{:S(2)}) copy-start(s32[4]{0:T(128)} %param.9) | copy-start | bytes 52
  9.4 1.9 %collective-permute-start.1 = (bf16[96,1152]{1,0:T(8,128)(2,1)S(1)}, bf16[96,1152]{1,0:T(8,128)(2,1)S(1)}, u32[]{:S(2)}, u32[]{:S(2)}) collective-permute-start(bf16[96,1152]{1,0:T(8,128)(2,1)S(1)} %offer.1), channel_id=1, source_target_pairs={{0,1},{1,0},{2,3},{3,2},{4,5},{5,4},{6,7},{7,6},{8,9},{9,8},{10,11... | collective-permute-start | bytes 663560 | tf_op jit(solution)/shard_map/ppermute | solution.py:23
  9.5 15.9 %collective-permute-start.5 = (bf16[200,1152]{1,0:T(8,128)(2,1)S(1)}, bf16[200,1152]{1,0:T(8,128)(2,1)S(1)}, u32[]{:S(2)}, u32[]{:S(2)}) collective-permute-start(bf16[200,1152]{1,0:T(8,128)(2,1)S(1)} %pad_maximum_fusion), channel_id=1, source_target_pairs={{0,4},{4,0},{8,12},{12,8},{16,20},{20,16},{24,28},{28,24},{1,5},{5... | collective-permute-start | bytes 1382408 | tf_op jit(solution)/shard_map/ppermute | solution.py:23
  11.5 13.9 %collective-permute-start.4 = (bf16[96,1152]{1,0:T(8,128)(2,1)S(1)}, bf16[96,1152]{1,0:T(8,128)(2,1)S(1)}, u32[]{:S(2)}, u32[]{:S(2)}) collective-permute-start(bf16[96,1152]{1,0:T(8,128)(2,1)S(1)} %choose.1.refs_0_), channel_id=1, source_target_pairs={{0,8},{4,12},{8,0},{12,4},{16,24},{20,28},{24,16},{28,20},{1,9},{5... | collective-permute-start | bytes 663560 | tf_op jit(solution)/shard_map/ppermute | solution.py:23
  13.1 12.9 %collective-permute-start.3 = (bf16[96,1152]{1,0:T(8,128)(2,1)S(1)}, bf16[96,1152]{1,0:T(8,128)(2,1)S(1)}, u32[]{:S(2)}, u32[]{:S(2)}) collective-permute-start(bf16[96,1152]{1,0:T(8,128)(2,1)S(1)} %choose.1.refs_0_), channel_id=1, source_target_pairs={{0,16},{4,20},{8,24},{12,28},{16,0},{20,4},{24,8},{28,12},{1,17},{... | collective-permute-start | bytes 663560 | tf_op jit(solution)/shard_map/ppermute | solution.py:23
  26.0 10.9 %collective-permute-start.6 = (bf16[96,1152]{1,0:T(8,128)(2,1)S(1)}, bf16[96,1152]{1,0:T(8,128)(2,1)S(1)}, u32[]{:S(2)}, u32[]{:S(2)}) collective-permute-start(bf16[96,1152]{1,0:T(8,128)(2,1)S(1)} %collective-permute-done.3.refs_1_), channel_id=1, source_target_pairs={{0,8},{4,12},{8,0},{12,4},{16,24},{20,28},{24,16},{28,20},{1,9},{5... | collective-permute-start | bytes 663560 | tf_op jit(solution)/shard_map/ppermute | solution.py:23
  26.5 13.3 %collective-permute-start.2 = (bf16[104,1152]{1,0:T(8,128)(2,1)S(1)}, bf16[104,1152]{1,0:T(8,128)(2,1)S(1)}, u32[]{:S(2)}, u32[]{:S(2)}) collective-permute-start(bf16[104,1152]{1,0:T(8,128)(2,1)S(1)} %scorer.1.refs_0_), channel_id=1, source_target_pairs={{0,16},{4,20},{8,24},{12,28},{16,0},{20,4},{24,8},{28,12},{1,17},{... | collective-permute-start | bytes 718856 | tf_op jit(solution)/shard_map/ppermute | solution.py:23
  38.0 15.0 %collective-permute-start.13 = (f32[80,1152]{1,0:T(8,128)S(1)}, f32[80,1152]{1,0:T(8,128)S(1)}, u32[]{:S(2)}, u32[]{:S(2)}) collective-permute-start(f32[80,1152]{1,0:T(8,128)S(1)} %slice.31), channel_id=1, source_target_pairs={{0,4},{4,0},{8,12},{12,8},{16,20},{20,16},{24,28},{28,24},{1,5},{5... | collective-permute-start | bytes 1105928 | tf_op jit(solution)/shard_map/ppermute | solution.py:23
  39.3 8.8 %collective-permute-start.7 = (bf16[104,1152]{1,0:T(8,128)(2,1)S(1)}, bf16[104,1152]{1,0:T(8,128)(2,1)S(1)}, u32[]{:S(2)}, u32[]{:S(2)}) collective-permute-start(bf16[104,1152]{1,0:T(8,128)(2,1)S(1)} %scorer.1.refs_0_), channel_id=1, source_target_pairs={{0,8},{4,12},{8,0},{12,4},{16,24},{20,28},{24,16},{28,20},{1,9},{5... | collective-permute-start | bytes 718856 | tf_op jit(solution)/shard_map/ppermute | solution.py:23
  39.8 11.9 %collective-permute-start.8 = (bf16[104,1152]{1,0:T(8,128)(2,1)S(1)}, bf16[104,1152]{1,0:T(8,128)(2,1)S(1)}, u32[]{:S(2)}, u32[]{:S(2)}) collective-permute-start(bf16[104,1152]{1,0:T(8,128)(2,1)S(1)} %collective-permute-done.2.refs_1_), channel_id=1, source_target_pairs={{0,8},{4,12},{8,0},{12,4},{16,24},{20,28},{24,16},{28,20},{1,9},{5... | collective-permute-start | bytes 718856 | tf_op jit(solution)/shard_map/ppermute | solution.py:23
  41.4 1.2 %collective-permute-start.9 = (f32[8,128]{1,0:T(8,128)S(1)}, f32[8,128]{1,0:T(8,128)S(1)}, u32[]{:S(2)}, u32[]{:S(2)}) collective-permute-start(f32[8,128]{1,0:T(8,128)S(1)} %get-tuple-element.24), channel_id=1, source_target_pairs={{0,1},{1,0},{2,3},{3,2},{4,5},{5,4},{6,7},{7,6},{8,9},{9,8},{10,11... | collective-permute-start | bytes 12296 | tf_op jit(solution)/shard_map/ppermute | solution.py:23
  42.5 3.6 %collective-permute-start.10 = (f32[8,128]{1,0:T(8,128)S(1)}, f32[8,128]{1,0:T(8,128)S(1)}, u32[]{:S(2)}, u32[]{:S(2)}) collective-permute-start(f32[8,128]{1,0:T(8,128)S(1)} %add.30), channel_id=1, source_target_pairs={{0,2},{1,3},{2,0},{3,1},{4,6},{5,7},{6,4},{7,5},{8,10},{9,11},{10,... | collective-permute-start | bytes 12296 | tf_op jit(solution)/shard_map/ppermute | solution.py:23
  48.1 3.6 %collective-permute-start.11 = (f32[8,128]{1,0:T(8,128)S(1)}, f32[8,128]{1,0:T(8,128)S(1)}, u32[]{:S(2)}, u32[]{:S(2)}) collective-permute-start(f32[8,128]{1,0:T(8,128)S(1)} %add.31), channel_id=1, source_target_pairs={{0,4},{4,0},{8,12},{12,8},{16,20},{20,16},{24,28},{28,24},{1,5},{5... | collective-permute-start | bytes 12296 | tf_op jit(solution)/shard_map/ppermute | solution.py:23
  49.7 5.3 %collective-permute-start.14 = (f32[16,1152]{1,0:T(8,128)S(1)}, f32[16,1152]{1,0:T(8,128)S(1)}, u32[]{:S(2)}, u32[]{:S(2)}) collective-permute-start(f32[16,1152]{1,0:T(8,128)S(1)} %slice.33), channel_id=1, source_target_pairs={{0,4},{4,0},{8,12},{12,8},{16,20},{20,16},{24,28},{28,24},{1,5},{5... | collective-permute-start | bytes 221192 | tf_op jit(solution)/shard_map/ppermute | solution.py:23
  52.2 11.5 %collective-permute-start.12 = (f32[96,1152]{1,0:T(8,128)S(1)}, f32[96,1152]{1,0:T(8,128)S(1)}, u32[]{:S(2)}, u32[]{:S(2)}) collective-permute-start(f32[96,1152]{1,0:T(8,128)S(1)} %text_side_mate.1), channel_id=1, source_target_pairs={{0,4},{4,0},{8,12},{12,8},{16,20},{20,16},{24,28},{28,24},{1,5},{5... | collective-permute-start | bytes 1327112 | tf_op jit(solution)/shard_map/ppermute | solution.py:23
  55.0 3.6 %collective-permute-start.15 = (f32[8,128]{1,0:T(8,128)S(1)}, f32[8,128]{1,0:T(8,128)S(1)}, u32[]{:S(2)}, u32[]{:S(2)}) collective-permute-start(f32[8,128]{1,0:T(8,128)S(1)} %add.32), channel_id=1, source_target_pairs={{0,8},{4,12},{8,0},{12,4},{16,24},{20,28},{24,16},{28,20},{1,9},{5... | collective-permute-start | bytes 12296 | tf_op jit(solution)/shard_map/ppermute | solution.py:23
  58.6 4.5 %collective-permute-start.16 = (f32[8,128]{1,0:T(8,128)S(1)}, f32[8,128]{1,0:T(8,128)S(1)}, u32[]{:S(2)}, u32[]{:S(2)}) collective-permute-start(f32[8,128]{1,0:T(8,128)S(1)} %add.34), channel_id=1, source_target_pairs={{0,16},{4,20},{8,24},{12,28},{16,0},{20,4},{24,8},{28,12},{1,17},{... | collective-permute-start | bytes 12296 | tf_op jit(solution)/shard_map/ppermute | solution.py:23

commit v4 on v3

--- a/solution.py
+++ b/solution.py
@@ -208,8 +208,7 @@
         cut = rows * 5 // 6
         first_grads = own_part[:cut] + along(mate_part[:cut], 1)
         rest_own, rest = own_part[cut:], mate_part[cut:]
-        total = hop_sum(total, hops[:2])
-        total = hop_sum(after(total, image_one_off), hops[2:3])
+        total = hop_sum(total, hops[:3])
         early_images = [scorer_image, image_two_off, image_one_off]
         early_part = call(functools.partial(text_kernel, 1, 3), [settings, mate[tailed:], *early_images], [grad_shape], "text_side_early")[0]
         rest = along(after(rest, early_part), 1)

time: 64.9 us -> 67.4 us (1.039)
  waiting for transfers between devices: 25.8 us -> 27.1 us
  starting transfers between devices: 20.4 us -> 21.6 us
    ppermute x17, waiting for transfers between devices: 25.8 us -> 27.1 us  [exchange(): lax.ppermute(array, axis, [(place, mate(place)) for place in range(size)])]
    ppermute x17, starting transfers between devices: 20.4 us -> 21.6 us  [exchange(): lax.ppermute(array, axis, [(place, mate(place)) for place in range(size)])]
where the time goes in v4:
time: 67.4 us; the launch traced here: 67.2 us
  waiting for transfers between devices  27.1 us (40%)
  starting transfers between devices  21.6 us (32%)
  blocking collectives  9.52 us (14%)
  Pallas kernels  4.89 us (7%)
  between operations  2.1 us (3%)
  other arithmetic  1.85 us (3%)
    ppermute x17, waiting for transfers between devices, exchange(): lax.ppermute(array, axis, [(place, mate(place)) for place in range(size)])  27.1 us
    ppermute x17, starting transfers between devices, exchange(): lax.ppermute(array, axis, [(place, mate(place)) for place in range(size)])  21.6 us
    all_gather x1, blocking collectives, shards(): group_images = lax.all_gather(after(packed[:tailed], partner_text), 'group')  9.52 us
    pallas_call x8, Pallas kernels, call(): pl.pallas_call(kernel, out_shape=[jax.ShapeDtypeStruct(shape, dtype) for...  4.89 us
  transfers between devices with their start and end apart: 17, of which 11 were waited for; matrix products, arithmetic and copies ran while one was open for 3% of the time, Pallas kernels for 6%

profile of v4, /device:TPU:0, one launch (start us, length us, event | category | flops | bytes accessed | tf_op | source)
XLA Modules:
  0.0 67.2 jit_solution(17712824667926455637)
XLA Ops:
  0.6 3.0 %collective-permute-start = (bf16[96,1152]{1,0:T(8,128)(2,1)}, bf16[96,1152]{1,0:T(8,128)(2,1)S(1)}, u32[]{:S(2)}, u32[]{:S(2)}) collective-permute-start(bf16[96,1152]{1,0:T(8,128)(2,1)} %bitcast.14), channel_id=1, source_target_pairs={{0,2},{1,3},{2,0},{3,1},{4,6},{5,7},{6,4},{7,5},{8,10},{9,11},{10,... | collective-permute-start | bytes 663560 | tf_op jit(solution)/shard_map/ppermute | solution.py:23
  5.0 0.1 maximum_bitcast_fusion.settings
  5.1 1.1 %pad_maximum_fusion = bf16[200,1152]{1,0:T(8,128)(2,1)S(1)} fusion(bf16[96,1152]{1,0:T(8,128)(2,1)} %bitcast.15, bf16[8,1152]{1,0:T(8,128)(2,1)S(1)} %fusion.5, bf16[96,1152]{1,0:T(8,128)(2,1)} %bitcast.13), kind=kLoop, calls=%fused_computation | loop fusion | flops 1382400 | bytes 921600 | tf_op jit(solution)/shard_map/concatenate | solution.py:174
  6.2 0.0 copy-start
  6.2 3.1 %collective-permute-done.across = bf16[96,1152]{1,0:T(8,128)(2,1)S(1)} collective-permute-done((bf16[96,1152]{1,0:T(8,128)(2,1)}, bf16[96,1152]{1,0:T(8,128)(2,1)S(1)}, u32[]{:S(2)}, u32[]{:S(2)}) %collective-permute-start) | collective-permute-done | bytes 221216 | tf_op jit(solution)/shard_map/ppermute | solution.py:23
  9.3 0.1 offer.1
  9.4 0.1 collective-permute-start.1
  9.5 1.8 %collective-permute-start.5 = (bf16[200,1152]{1,0:T(8,128)(2,1)S(1)}, bf16[200,1152]{1,0:T(8,128)(2,1)S(1)}, u32[]{:S(2)}, u32[]{:S(2)}) collective-permute-start(bf16[200,1152]{1,0:T(8,128)(2,1)S(1)} %pad_maximum_fusion), channel_id=1, source_target_pairs={{0,4},{4,0},{8,12},{12,8},{16,20},{20,16},{24,28},{28,24},{1,5},{5... | collective-permute-start | bytes 1382408 | tf_op jit(solution)/shard_map/ppermute | solution.py:23
  11.3 0.0 collective-permute-done.1.offered
  11.3 0.1 choose.1.refs_0_
  11.5 1.6 %collective-permute-start.4 = (bf16[96,1152]{1,0:T(8,128)(2,1)S(1)}, bf16[96,1152]{1,0:T(8,128)(2,1)S(1)}, u32[]{:S(2)}, u32[]{:S(2)}) collective-permute-start(bf16[96,1152]{1,0:T(8,128)(2,1)S(1)} %choose.1.refs_0_), channel_id=1, source_target_pairs={{0,8},{4,12},{8,0},{12,4},{16,24},{20,28},{24,16},{28,20},{1,9},{5... | collective-permute-start | bytes 663560 | tf_op jit(solution)/shard_map/ppermute | solution.py:23
  13.1 2.6 %collective-permute-start.3 = (bf16[96,1152]{1,0:T(8,128)(2,1)S(1)}, bf16[96,1152]{1,0:T(8,128)(2,1)S(1)}, u32[]{:S(2)}, u32[]{:S(2)}) collective-permute-start(bf16[96,1152]{1,0:T(8,128)(2,1)S(1)} %choose.1.refs_0_), channel_id=1, source_target_pairs={{0,16},{4,20},{8,24},{12,28},{16,0},{20,4},{24,8},{28,12},{1,17},{... | collective-permute-start | bytes 663560 | tf_op jit(solution)/shard_map/ppermute | solution.py:23
  15.7 9.5 %all-gather = bf16[416,1152]{1,0:T(8,128)(2,1)S(1)} all-gather(bf16[104,1152]{1,0:T(8,128)(2,1)S(1)} %slice.27.images), channel_id=2, replica_groups=mesh['blk'=8,'group'=4] {'group'}, dimensions={0}, use_global_device_ids=true | all-gather | bytes 1198080 | tf_op jit(solution)/shard_map/all_gather | solution.py:184
  25.2 0.2 scorer.1.refs_0_
  25.4 0.0 collective-permute-done.5
  25.4 0.0 collective-permute-done.4.refs_2_
  25.4 0.6 collective-permute-done.3.refs_1_
  26.0 0.4 collective-permute-start.6
  26.5 2.6 %collective-permute-start.2 = (bf16[104,1152]{1,0:T(8,128)(2,1)S(1)}, bf16[104,1152]{1,0:T(8,128)(2,1)S(1)}, u32[]{:S(2)}, u32[]{:S(2)}) collective-permute-start(bf16[104,1152]{1,0:T(8,128)(2,1)S(1)} %scorer.1.refs_0_), channel_id=1, source_target_pairs={{0,16},{4,20},{8,24},{12,28},{16,0},{20,4},{24,8},{28,12},{1,17},{... | collective-permute-start | bytes 718856 | tf_op jit(solution)/shard_map/ppermute | solution.py:23
  29.1 7.8 %collective-permute-done.6.refs_3_ = bf16[96,1152]{1,0:T(8,128)(2,1)S(1)} collective-permute-done((bf16[96,1152]{1,0:T(8,128)(2,1)S(1)}, bf16[96,1152]{1,0:T(8,128)(2,1)S(1)}, u32[]{:S(2)}, u32[]{:S(2)}) %collective-permute-start.6) | collective-permute-done | bytes 221216 | tf_op jit(solution)/shard_map/ppermute | solution.py:23
  36.9 1.0 %image_side.1 = (f32[96,1152]{1,0:T(8,128)S(1)}, f32[96,1152]{1,0:T(8,128)S(1)}, f32[8,128]{1,0:T(8,128)S(1)}) custom-call(f32[1,2]{1,0:T(1,128)S(1)} %maximum_bitcast_fusion.settings, bf16[104,1152]{1,0:T(8,128)(2,1)S(1)} %slice.27.images, bf16[104,1152]{1,0:T(8,128)(2,1)S(1)} %slice.34.mate, bf16[96,1152]{1,0:T(8,128)(2,1)S(1)} %choose.1.refs_0_, ...), custom_call_target="tpu_custom_call" | custom-call | tf_op jit(solution)/shard_map/image_side/pallas_call | solution.py:138
  38.0 1.4 %collective-permute-start.13 = (f32[80,1152]{1,0:T(8,128)S(1)}, f32[80,1152]{1,0:T(8,128)S(1)}, u32[]{:S(2)}, u32[]{:S(2)}) collective-permute-start(f32[80,1152]{1,0:T(8,128)S(1)} %slice.31), channel_id=1, source_target_pairs={{0,4},{4,0},{8,12},{12,8},{16,20},{20,16},{24,28},{28,24},{1,5},{5... | collective-permute-start | bytes 1105928 | tf_op jit(solution)/shard_map/ppermute | solution.py:23
  39.3 0.5 collective-permute-done.2.refs_1_
  39.8 0.0 collective-permute-start.8
  39.8 2.0 %collective-permute-start.7 = (bf16[104,1152]{1,0:T(8,128)(2,1)S(1)}, bf16[104,1152]{1,0:T(8,128)(2,1)S(1)}, u32[]{:S(2)}, u32[]{:S(2)}) collective-permute-start(bf16[104,1152]{1,0:T(8,128)(2,1)S(1)} %scorer.1.refs_0_), channel_id=1, source_target_pairs={{0,8},{4,12},{8,0},{12,4},{16,24},{20,28},{24,16},{28,20},{1,9},{5... | collective-permute-start | bytes 718856 | tf_op jit(solution)/shard_map/ppermute | solution.py:23
  41.9 0.0 collective-permute-start.9
  41.9 1.2 %collective-permute-done.9 = f32[8,128]{1,0:T(8,128)S(1)} collective-permute-done((f32[8,128]{1,0:T(8,128)S(1)}, f32[8,128]{1,0:T(8,128)S(1)}, u32[]{:S(2)}, u32[]{:S(2)}) %collective-permute-start.9) | collective-permute-done | bytes 4128 | tf_op jit(solution)/shard_map/ppermute | solution.py:23
  43.0 1.0 %collective-permute-start.10 = (f32[8,128]{1,0:T(8,128)S(1)}, f32[8,128]{1,0:T(8,128)S(1)}, u32[]{:S(2)}, u32[]{:S(2)}) collective-permute-start(f32[8,128]{1,0:T(8,128)S(1)} %add.30), channel_id=1, source_target_pairs={{0,2},{1,3},{2,0},{3,1},{4,6},{5,7},{6,4},{7,5},{8,10},{9,11},{10,... | collective-permute-start | bytes 12296 | tf_op jit(solution)/shard_map/ppermute | solution.py:23
  44.0 2.6 %collective-permute-done.10 = f32[8,128]{1,0:T(8,128)S(1)} collective-permute-done((f32[8,128]{1,0:T(8,128)S(1)}, f32[8,128]{1,0:T(8,128)S(1)}, u32[]{:S(2)}, u32[]{:S(2)}) %collective-permute-start.10) | collective-permute-done | bytes 4128 | tf_op jit(solution)/shard_map/ppermute | solution.py:23
  46.6 1.4 %collective-permute-start.11 = (f32[8,128]{1,0:T(8,128)S(1)}, f32[8,128]{1,0:T(8,128)S(1)}, u32[]{:S(2)}, u32[]{:S(2)}) collective-permute-start(f32[8,128]{1,0:T(8,128)S(1)} %add.31), channel_id=1, source_target_pairs={{0,4},{4,0},{8,12},{12,8},{16,20},{20,16},{24,28},{28,24},{1,5},{5... | collective-permute-start | bytes 12296 | tf_op jit(solution)/shard_map/ppermute | solution.py:23
  48.0 2.2 %collective-permute-done.11 = f32[8,128]{1,0:T(8,128)S(1)} collective-permute-done((f32[8,128]{1,0:T(8,128)S(1)}, f32[8,128]{1,0:T(8,128)S(1)}, u32[]{:S(2)}, u32[]{:S(2)}) %collective-permute-start.11) | collective-permute-done | bytes 4128 | tf_op jit(solution)/shard_map/ppermute | solution.py:23
  50.2 0.0 collective-permute-done.8.refs_3_.refs_0_
  50.2 0.7 collective-permute-done.7.refs_2_
  50.9 0.8 %text_side_early.1.refs_1_ = f32[96,1152]{1,0:T(8,128)S(1)} custom-call(f32[1,2]{1,0:T(1,128)S(1)} %maximum_bitcast_fusion.settings, bf16[96,1152]{1,0:T(8,128)(2,1)S(1)} %slice.35.texts, bf16[104,1152]{1,0:T(8,128)(2,1)S(1)} %scorer.1.refs_0_, bf16[104,1152]{1,0:T(8,128)(2,1)S(1)} %collective-permute-done.2.refs_1_, ...), custom_call_target="tpu_custom_call" | custom-call | tf_op jit(solution)/shard_map/text_side_early/pallas_call | solution.py:138
  51.7 0.5 text_side_mate.1
  52.2 1.9 %collective-permute-start.14 = (f32[16,1152]{1,0:T(8,128)S(1)}, f32[16,1152]{1,0:T(8,128)S(1)}, u32[]{:S(2)}, u32[]{:S(2)}) collective-permute-start(f32[16,1152]{1,0:T(8,128)S(1)} %slice.33), channel_id=1, source_target_pairs={{0,4},{4,0},{8,12},{12,8},{16,20},{20,16},{24,28},{28,24},{1,5},{5... | collective-permute-start | bytes 221192 | tf_op jit(solution)/shard_map/ppermute | solution.py:23
  54.1 0.2 collective-permute-start.12
  54.3 0.0 collective-permute-done.13
  54.3 0.1 slice_add_fusion.first
  54.4 3.1 %collective-permute-done.14.rest = f32[16,1152]{1,0:T(8,128)S(1)} collective-permute-done((f32[16,1152]{1,0:T(8,128)S(1)}, f32[16,1152]{1,0:T(8,128)S(1)}, u32[]{:S(2)}, u32[]{:S(2)}) %collective-permute-start.14) | collective-permute-done | bytes 73760 | tf_op jit(solution)/shard_map/ppermute | solution.py:23
  57.5 0.3 collective-permute-start.15
  57.8 1.1 %text_side_own.1.own_text = f32[96,1152]{1,0:T(8,128)S(1)} custom-call(f32[1,2]{1,0:T(1,128)S(1)} %maximum_bitcast_fusion.settings, bf16[96,1152]{1,0:T(8,128)(2,1)S(1)} %slice.26.own.texts, bf16[104,1152]{1,0:T(8,128)(2,1)S(1)} %scorer.1.refs_0_, bf16[104,1152]{1,0:T(8,128)(2,1)S(1)} %collective-permute-done.2.refs_1_, ...), custom_call_target="tpu_custom_call" | custom-call | tf_op jit(solution)/shard_map/text_side_own/pallas_call | solution.py:138
  58.9 2.2 %collective-permute-done.15 = f32[8,128]{1,0:T(8,128)S(1)} collective-permute-done((f32[8,128]{1,0:T(8,128)S(1)}, f32[8,128]{1,0:T(8,128)S(1)}, u32[]{:S(2)}, u32[]{:S(2)}) %collective-permute-start.15) | collective-permute-done | bytes 4128 | tf_op jit(solution)/shard_map/ppermute | solution.py:23
  61.1 1.4 %collective-permute-start.16 = (f32[8,128]{1,0:T(8,128)S(1)}, f32[8,128]{1,0:T(8,128)S(1)}, u32[]{:S(2)}, u32[]{:S(2)}) collective-permute-start(f32[8,128]{1,0:T(8,128)S(1)} %add.34), channel_id=1, source_target_pairs={{0,16},{4,20},{8,24},{12,28},{16,0},{20,4},{24,8},{28,12},{1,17},{... | collective-permute-start | bytes 12296 | tf_op jit(solution)/shard_map/ppermute | solution.py:23
  62.5 3.1 %collective-permute-done.16 = f32[8,128]{1,0:T(8,128)S(1)} collective-permute-done((f32[8,128]{1,0:T(8,128)S(1)}, f32[8,128]{1,0:T(8,128)S(1)}, u32[]{:S(2)}, u32[]{:S(2)}) %collective-permute-start.16) | collective-permute-done | bytes 4128 | tf_op jit(solution)/shard_map/ppermute | solution.py:23
  65.6 0.6 multiply_reduce_fusion
  66.2 0.0 collective-permute-done.12.text_part
  66.2 1.0 %finish.1 = (f32[96,1152]{1,0:T(8,128)}, f32[96,1152]{1,0:T(8,128)}) custom-call(f32[96,1152]{1,0:T(8,128)S(1)} %text_side_own.1.own_text, f32[96,1152]{1,0:T(8,128)S(1)} %collective-permute-done.12.text_part, f32[80,1152]{1,0:T(8,128)S(1)} %slice_add_fusion.first, f32[16,1152]{1,0:T(8,128)S(1)} %slice.32.rest_own, f32[16,1152]{1,0:T(8,128)S(1)} %collective-permute-done.14.rest), custom_call_target="tpu_custom_call" | custom-call | tf_op jit(solution)/shard_map/finish/pallas_call | solution.py:138
  (16 shorter events, 0.2 us)
Async XLA Ops:
  0.6 8.6 %collective-permute-start = (bf16[96,1152]{1,0:T(8,128)(2,1)}, bf16[96,1152]{1,0:T(8,128)(2,1)S(1)}, u32[]{:S(2)}, u32[]{:S(2)}) collective-permute-start(bf16[96,1152]{1,0:T(8,128)(2,1)} %bitcast.14), channel_id=1, source_target_pairs={{0,2},{1,3},{2,0},{3,1},{4,6},{5,7},{6,4},{7,5},{8,10},{9,11},{10,... | collective-permute-start | bytes 663560 | tf_op jit(solution)/shard_map/ppermute | solution.py:23
  4.3 0.7 copy-start.1
  6.2 3.1 %copy-start = (s32[4]{0:T(128)S(1)}, s32[4]{0:T(128)}, u32[]{:S(2)}) copy-start(s32[4]{0:T(128)} %param.9) | copy-start | bytes 52
  9.4 1.9 %collective-permute-start.1 = (bf16[96,1152]{1,0:T(8,128)(2,1)S(1)}, bf16[96,1152]{1,0:T(8,128)(2,1)S(1)}, u32[]{:S(2)}, u32[]{:S(2)}) collective-permute-start(bf16[96,1152]{1,0:T(8,128)(2,1)S(1)} %offer.1), channel_id=1, source_target_pairs={{0,1},{1,0},{2,3},{3,2},{4,5},{5,4},{6,7},{7,6},{8,9},{9,8},{10,11... | collective-permute-start | bytes 663560 | tf_op jit(solution)/shard_map/ppermute | solution.py:23
  9.5 15.9 %collective-permute-start.5 = (bf16[200,1152]{1,0:T(8,128)(2,1)S(1)}, bf16[200,1152]{1,0:T(8,128)(2,1)S(1)}, u32[]{:S(2)}, u32[]{:S(2)}) collective-permute-start(bf16[200,1152]{1,0:T(8,128)(2,1)S(1)} %pad_maximum_fusion), channel_id=1, source_target_pairs={{0,4},{4,0},{8,12},{12,8},{16,20},{20,16},{24,28},{28,24},{1,5},{5... | collective-permute-start | bytes 1382408 | tf_op jit(solution)/shard_map/ppermute | solution.py:23
  11.5 13.9 %collective-permute-start.4 = (bf16[96,1152]{1,0:T(8,128)(2,1)S(1)}, bf16[96,1152]{1,0:T(8,128)(2,1)S(1)}, u32[]{:S(2)}, u32[]{:S(2)}) collective-permute-start(bf16[96,1152]{1,0:T(8,128)(2,1)S(1)} %choose.1.refs_0_), channel_id=1, source_target_pairs={{0,8},{4,12},{8,0},{12,4},{16,24},{20,28},{24,16},{28,20},{1,9},{5... | collective-permute-start | bytes 663560 | tf_op jit(solution)/shard_map/ppermute | solution.py:23
  13.1 12.9 %collective-permute-start.3 = (bf16[96,1152]{1,0:T(8,128)(2,1)S(1)}, bf16[96,1152]{1,0:T(8,128)(2,1)S(1)}, u32[]{:S(2)}, u32[]{:S(2)}) collective-permute-start(bf16[96,1152]{1,0:T(8,128)(2,1)S(1)} %choose.1.refs_0_), channel_id=1, source_target_pairs={{0,16},{4,20},{8,24},{12,28},{16,0},{20,4},{24,8},{28,12},{1,17},{... | collective-permute-start | bytes 663560 | tf_op jit(solution)/shard_map/ppermute | solution.py:23
  26.0 10.9 %collective-permute-start.6 = (bf16[96,1152]{1,0:T(8,128)(2,1)S(1)}, bf16[96,1152]{1,0:T(8,128)(2,1)S(1)}, u32[]{:S(2)}, u32[]{:S(2)}) collective-permute-start(bf16[96,1152]{1,0:T(8,128)(2,1)S(1)} %collective-permute-done.3.refs_1_), channel_id=1, source_target_pairs={{0,8},{4,12},{8,0},{12,4},{16,24},{20,28},{24,16},{28,20},{1,9},{5... | collective-permute-start | bytes 663560 | tf_op jit(solution)/shard_map/ppermute | solution.py:23
  26.5 13.3 %collective-permute-start.2 = (bf16[104,1152]{1,0:T(8,128)(2,1)S(1)}, bf16[104,1152]{1,0:T(8,128)(2,1)S(1)}, u32[]{:S(2)}, u32[]{:S(2)}) collective-permute-start(bf16[104,1152]{1,0:T(8,128)(2,1)S(1)} %scorer.1.refs_0_), channel_id=1, source_target_pairs={{0,16},{4,20},{8,24},{12,28},{16,0},{20,4},{24,8},{28,12},{1,17},{... | collective-permute-start | bytes 718856 | tf_op jit(solution)/shard_map/ppermute | solution.py:23
  38.0 16.4 %collective-permute-start.13 = (f32[80,1152]{1,0:T(8,128)S(1)}, f32[80,1152]{1,0:T(8,128)S(1)}, u32[]{:S(2)}, u32[]{:S(2)}) collective-permute-start(f32[80,1152]{1,0:T(8,128)S(1)} %slice.31), channel_id=1, source_target_pairs={{0,4},{4,0},{8,12},{12,8},{16,20},{20,16},{24,28},{28,24},{1,5},{5... | collective-permute-start | bytes 1105928 | tf_op jit(solution)/shard_map/ppermute | solution.py:23
  39.8 10.4 %collective-permute-start.8 = (bf16[104,1152]{1,0:T(8,128)(2,1)S(1)}, bf16[104,1152]{1,0:T(8,128)(2,1)S(1)}, u32[]{:S(2)}, u32[]{:S(2)}) collective-permute-start(bf16[104,1152]{1,0:T(8,128)(2,1)S(1)} %collective-permute-done.2.refs_1_), channel_id=1, source_target_pairs={{0,8},{4,12},{8,0},{12,4},{16,24},{20,28},{24,16},{28,20},{1,9},{5... | collective-permute-start | bytes 718856 | tf_op jit(solution)/shard_map/ppermute | solution.py:23
  39.8 11.1 %collective-permute-start.7 = (bf16[104,1152]{1,0:T(8,128)(2,1)S(1)}, bf16[104,1152]{1,0:T(8,128)(2,1)S(1)}, u32[]{:S(2)}, u32[]{:S(2)}) collective-permute-start(bf16[104,1152]{1,0:T(8,128)(2,1)S(1)} %scorer.1.refs_0_), channel_id=1, source_target_pairs={{0,8},{4,12},{8,0},{12,4},{16,24},{20,28},{24,16},{28,20},{1,9},{5... | collective-permute-start | bytes 718856 | tf_op jit(solution)/shard_map/ppermute | solution.py:23
  41.9 1.2 %collective-permute-start.9 = (f32[8,128]{1,0:T(8,128)S(1)}, f32[8,128]{1,0:T(8,128)S(1)}, u32[]{:S(2)}, u32[]{:S(2)}) collective-permute-start(f32[8,128]{1,0:T(8,128)S(1)} %get-tuple-element.23), channel_id=1, source_target_pairs={{0,1},{1,0},{2,3},{3,2},{4,5},{5,4},{6,7},{7,6},{8,9},{9,8},{10,11... | collective-permute-start | bytes 12296 | tf_op jit(solution)/shard_map/ppermute | solution.py:23
  43.0 3.6 %collective-permute-start.10 = (f32[8,128]{1,0:T(8,128)S(1)}, f32[8,128]{1,0:T(8,128)S(1)}, u32[]{:S(2)}, u32[]{:S(2)}) collective-permute-start(f32[8,128]{1,0:T(8,128)S(1)} %add.30), channel_id=1, source_target_pairs={{0,2},{1,3},{2,0},{3,1},{4,6},{5,7},{6,4},{7,5},{8,10},{9,11},{10,... | collective-permute-start | bytes 12296 | tf_op jit(solution)/shard_map/ppermute | solution.py:23
  46.6 3.6 %collective-permute-start.11 = (f32[8,128]{1,0:T(8,128)S(1)}, f32[8,128]{1,0:T(8,128)S(1)}, u32[]{:S(2)}, u32[]{:S(2)}) collective-permute-start(f32[8,128]{1,0:T(8,128)S(1)} %add.31), channel_id=1, source_target_pairs={{0,4},{4,0},{8,12},{12,8},{16,20},{20,16},{24,28},{28,24},{1,5},{5... | collective-permute-start | bytes 12296 | tf_op jit(solution)/shard_map/ppermute | solution.py:23
  52.2 5.3 %collective-permute-start.14 = (f32[16,1152]{1,0:T(8,128)S(1)}, f32[16,1152]{1,0:T(8,128)S(1)}, u32[]{:S(2)}, u32[]{:S(2)}) collective-permute-start(f32[16,1152]{1,0:T(8,128)S(1)} %slice.33), channel_id=1, source_target_pairs={{0,4},{4,0},{8,12},{12,8},{16,20},{20,16},{24,28},{28,24},{1,5},{5... | collective-permute-start | bytes 221192 | tf_op jit(solution)/shard_map/ppermute | solution.py:23
  54.1 12.1 %collective-permute-start.12 = (f32[96,1152]{1,0:T(8,128)S(1)}, f32[96,1152]{1,0:T(8,128)S(1)}, u32[]{:S(2)}, u32[]{:S(2)}) collective-permute-start(f32[96,1152]{1,0:T(8,128)S(1)} %text_side_mate.1), channel_id=1, source_target_pairs={{0,4},{4,0},{8,12},{12,8},{16,20},{20,16},{24,28},{28,24},{1,5},{5... | collective-permute-start | bytes 1327112 | tf_op jit(solution)/shard_map/ppermute | solution.py:23
  57.5 3.6 %collective-permute-start.15 = (f32[8,128]{1,0:T(8,128)S(1)}, f32[8,128]{1,0:T(8,128)S(1)}, u32[]{:S(2)}, u32[]{:S(2)}) collective-permute-start(f32[8,128]{1,0:T(8,128)S(1)} %add.32), channel_id=1, source_target_pairs={{0,8},{4,12},{8,0},{12,4},{16,24},{20,28},{24,16},{28,20},{1,9},{5... | collective-permute-start | bytes 12296 | tf_op jit(solution)/shard_map/ppermute | solution.py:23
  61.1 4.5 %collective-permute-start.16 = (f32[8,128]{1,0:T(8,128)S(1)}, f32[8,128]{1,0:T(8,128)S(1)}, u32[]{:S(2)}, u32[]{:S(2)}) collective-permute-start(f32[8,128]{1,0:T(8,128)S(1)} %add.34), channel_id=1, source_target_pairs={{0,16},{4,20},{8,24},{12,28},{16,0},{20,4},{24,8},{28,12},{1,17},{... | collective-permute-start | bytes 12296 | tf_op jit(solution)/shard_map/ppermute | solution.py:23
